TPU v7x, 32 devices: a whole 2x2x4 slice. The times are simulated.
32 devices in a mesh: ctx: 16 (over z, y, core), fsdp: 2 (over x).
Axes of the slice: x: 2, y: 2, z: 4, core: 2. Of those that a mesh axis runs over, the one named last changes fastest.
Arguments:
- hidden: bfloat16 [2, 4096, 5376], P('fsdp', 'ctx'), may hold values from -6 to 6
- queries: bfloat16 [2, 4096, 2048], P('fsdp', 'ctx'), may hold values from -23 to 23
- key_heads: bfloat16 [2, 4096, 1024], P('fsdp', 'ctx'), may hold values from -6 to 6
- w_value: bfloat16 [5376, 1024], P('fsdp'), may hold values from -0.078125 to 0.078125
- d_out: bfloat16 [2, 4096, 2048], P('fsdp', 'ctx'), may hold values from -6 to 6
- segments: int32 [2, 4096], P('fsdp', 'ctx'), may hold values from 0 to 3, never falling along the last dimension, each value on 1 to 2048 neighbouring positions
Outputs:
- attn_out: bfloat16 [2, 4096, 2048], P('fsdp', 'ctx')
- d_queries: bfloat16 [2, 4096, 2048], P('fsdp', 'ctx')
- d_keys: bfloat16 [2, 4096, 1024], P('fsdp', 'ctx')
- d_hidden: bfloat16 [2, 4096, 5376], P('fsdp', 'ctx')
- d_w_value: float32 [5376, 1024], P(('ctx', 'fsdp'))
Inputs may be any that keep to these rules, and one draw needn't show every extreme that they name: `segments`: document ids never fall along a sequence; a document holds at most half of the 4096 tokens.
All inputs are finite; a program needn't handle non-finite values.
Results may differ from a plain program's by a relative error of at most 0.024.
Values may be sent and summed in bfloat16 or wider, within the bound.
No kernel may reach another device: no remote copies, remote signals or barrier semaphores. Data moves between devices by JAX's collectives and lax.ppermute only.
A program may use at most 256 MiB of HBM per device.

v0:
```python
import math

import jax
import jax.numpy as jnp
from jax import lax
from jax.sharding import PartitionSpec as P

HQ = 16
HK = 8
HD = 128
WINDOW = 1024
GROUP = 2


score_scale = 1.0 / math.sqrt(168.0)


def shifted(x, axis, by):
    length = lax.axis_size(axis)
    pairs = [(i, i + by) for i in range(length) if 0 <= i + by < length]
    return lax.ppermute(x, axis, pairs)


def shards(hidden, queries, key_heads, w_value, d_out, segments):
    shard_rows = hidden.shape[1]
    kv_width = w_value.shape[1]
    n_hops = WINDOW // shard_rows
    span_rows = (n_hops + 1) * shard_rows
    tokens_in = hidden[0]
    query_rows = queries[0].reshape(shard_rows, HK, GROUP, HD)
    own_keys = key_heads[0]
    own_segments = segments[0]
    grad_heads = d_out[0].reshape(shard_rows, HK, GROUP, HD)
    w_full = lax.all_gather(w_value, "fsdp", axis=0, tiled=True)
    values = jnp.dot(tokens_in, w_full, preferred_element_type=jnp.float32).astype(jnp.bfloat16)
    segment_tags = own_segments.astype(jnp.bfloat16)
    arrived = []
    for hop_index in range(1, n_hops + 1):
        arrived.append(shifted((own_keys, values, segment_tags), "ctx", hop_index))
    ordered = arrived[::-1] + [(own_keys, values, segment_tags)]
    window_keys = jnp.concatenate([parcel[0] for parcel in ordered], 0).reshape(span_rows, HK, HD)
    window_values = jnp.concatenate([parcel[1] for parcel in ordered], 0).reshape(span_rows, HK, HD)
    window_tags = jnp.concatenate([parcel[2] for parcel in ordered], 0).astype(jnp.float32)
    first_query = lax.axis_index("ctx") * shard_rows
    query_pos = first_query + jnp.arange(shard_rows, dtype=jnp.int32)
    key_pos = first_query - WINDOW + jnp.arange(span_rows, dtype=jnp.int32)
    distance = query_pos[:, None] - key_pos[None, :]
    allowed = (
        (own_segments.astype(jnp.float32)[:, None] == window_tags[None, :])
        & (distance >= 0)
        & (distance < WINDOW)
        & (key_pos[None, :] >= 0)
    )
    scores = (
        jnp.einsum("tgrd,lgd->grtl", query_rows, window_keys, preferred_element_type=jnp.float32)
        * score_scale
    )
    scores = jnp.where(allowed, scores, -jnp.inf)
    highest = jnp.max(scores, axis=-1, keepdims=True)
    raw_weights = jnp.exp(scores - highest)
    probs = raw_weights / jnp.sum(raw_weights, axis=-1, keepdims=True)
    probs_low = probs.astype(jnp.bfloat16)
    out_heads = jnp.einsum(
        "grtl,lgd->tgrd", probs_low, window_values, preferred_element_type=jnp.float32
    ).astype(jnp.bfloat16)
    grad_probs = jnp.einsum(
        "tgrd,lgd->grtl", grad_heads, window_values, preferred_element_type=jnp.float32
    )
    delta_sum = jnp.sum(grad_heads.astype(jnp.float32) * out_heads.astype(jnp.float32), axis=-1)
    delta_sum = jnp.transpose(delta_sum, (1, 2, 0))[..., None]
    grad_scores = (probs * (grad_probs - delta_sum)).astype(jnp.bfloat16)
    d_query_heads = (
        score_scale
        * jnp.einsum("grtl,lgd->tgrd", grad_scores, window_keys, preferred_element_type=jnp.float32)
    ).astype(jnp.bfloat16)
    key_terms = (
        (
            score_scale
            * jnp.einsum(
                "grtl,tgrd->lgd", grad_scores, query_rows, preferred_element_type=jnp.float32
            )
        )
        .astype(jnp.bfloat16)
        .reshape(span_rows, kv_width)
    )
    value_terms = (
        jnp.einsum("grtl,tgrd->lgd", probs_low, grad_heads, preferred_element_type=jnp.float32)
        .astype(jnp.bfloat16)
        .reshape(span_rows, kv_width)
    )
    own_start = n_hops * shard_rows
    key_total = key_terms[own_start:].astype(jnp.float32)
    value_total = value_terms[own_start:].astype(jnp.float32)
    for hop_index in range(1, n_hops + 1):
        low_edge = (n_hops - hop_index) * shard_rows
        back_keys, back_values = shifted(
            (
                key_terms[low_edge : low_edge + shard_rows],
                value_terms[low_edge : low_edge + shard_rows],
            ),
            "ctx",
            -hop_index,
        )
        key_total = key_total + back_keys.astype(jnp.float32)
        value_total = value_total + back_values.astype(jnp.float32)
    d_key_rows = key_total.astype(jnp.bfloat16)
    d_values_low = value_total.astype(jnp.bfloat16)
    d_tokens = lax.dot_general(
        d_values_low, w_full, (((1,), (1,)), ((), ())), preferred_element_type=jnp.float32
    ).astype(jnp.bfloat16)
    d_weight = lax.psum_scatter(
        lax.dot_general(
            tokens_in, d_values_low, (((0,), (0,)), ((), ())), preferred_element_type=jnp.float32
        ),
        ("ctx", "fsdp"),
        scatter_dimension=0,
        tiled=True,
    )
    return (
        out_heads.reshape(shard_rows, HQ * HD)[None],
        d_query_heads.reshape(shard_rows, HQ * HD)[None],
        d_key_rows[None],
        d_tokens[None],
        d_weight,
    )


def solution(mesh):
    in_specs = (
        P("fsdp", "ctx", None),
        P("fsdp", "ctx", None),
        P("fsdp", "ctx", None),
        P("fsdp", None),
        P("fsdp", "ctx", None),
        P("fsdp", "ctx"),
    )
    out_specs = (
        P("fsdp", "ctx", None),
        P("fsdp", "ctx", None),
        P("fsdp", "ctx", None),
        P("fsdp", "ctx", None),
        P(("ctx", "fsdp"), None),
    )
    return jax.shard_map(shards, mesh=mesh, in_specs=in_specs, out_specs=out_specs, check_vma=False)
```

profile of v0, /device:TPU:9, one launch (start us, length us, event | category | flops | bytes accessed | tf_op | source)
XLA Modules:
  0.0 445.8 jit_solution(532118718623357471)
XLA Ops:
  8.9 3.8 collective-permute-start.7
  12.8 3.1 collective-permute-start.6
  15.9 2.3 collective-permute-start.5
  18.2 3.2 collective-permute-start.4
  22.7 3.4 collective-permute-start.11
  27.2 2.4 copy.101
  29.6 2.5 copy.66
  32.0 2.8 collective-permute-start.10
  41.4 2.1 copy.61
  43.5 4.9 %collective-permute-done.10 = bf16[256,1024]{0,1:T(8,128)(2,1)} collective-permute-done((bf16[256,1024]{0,1:T(8,128)(2,1)S(1)}, bf16[256,1024]{0,1:T(8,128)(2,1)}, u32[]{:S(2)}, u32[]{:S(2)}) %collective-permute-start.10) | collective-permute-done | bytes 524320 | tf_op jit(solution)/shard_map/ppermute | solution.py:21
  48.4 2.0 copy.60
  50.5 9.8 %collective-permute-done.9 = bf16[256,1024]{0,1:T(8,128)(2,1)} collective-permute-done((bf16[256,1024]{0,1:T(8,128)(2,1)S(1)}, bf16[256,1024]{0,1:T(8,128)(2,1)}, u32[]{:S(2)}, u32[]{:S(2)}) %collective-permute-start.9) | collective-permute-done | bytes 524320 | tf_op jit(solution)/shard_map/ppermute | solution.py:21
  60.3 2.0 copy.59
  62.4 2.1 copy.58
  64.5 2.1 constant_dynamic-update-slice_fusion.9
  66.5 1.9 constant_dynamic-update-slice_fusion.8
  68.5 1.9 constant_dynamic-update-slice_fusion.7
  72.2 12.2 %exponential_reduce_fusion = (f32[8,2,256]{2,1,0:T(2,128)S(1)}, f32[8,2,256,1280]{2,3,1,0:T(8,128)}) fusion(bf16[256,8,2,128]{0,3,2,1:T(8,128)(2,1)} %bitcast.130, pred[256,1280]{0,1:T(8,128)(4,1)} %fusion.30, bf16[1280,8,128]{2,0,1:T(8,128)(2,1)} %constant_dynamic-update-slice_fusion.5), kind=kOutput, calls=%fused_computation.7 | convolution fusion | flops 1363150080 | bytes 24985600 | tf_op jit(solution)/shard_map/sub | solution.py:60
  84.5 14.4 %fusion.5 = bf16[8,2,256,1280]{2,3,1,0:T(8,128)(2,1)} fusion(f32[8,2,256]{2,1,0:T(2,128)S(1)} %get-tuple-element.30, f32[8,2,256,1280]{2,3,1,0:T(8,128)} %get-tuple-element.31), kind=kLoop, calls=%fused_computation.11 | loop fusion | flops 10485760 | bytes 31473664 | tf_op jit(solution)/shard_map/convert_element_type | solution.py:62
  98.8 9.0 %fusion.7 = bf16[1280,8,128]{0,2,1:T(8,128)(2,1)} fusion(bf16[8,2,256,1280]{2,3,1,0:T(8,128)(2,1)} %fusion.5, bf16[256,8,2,128]{0,3,2,1:T(8,128)(2,1)S(1)} %bitcast.115), kind=kOutput, calls=%fused_computation.15 | convolution fusion | flops 1343488000 | bytes 14155776 | tf_op jit(solution)/shard_map/grtl,tgrd->lgd/dot_general | solution.py:87
  111.6 9.7 %collective-permute-start.18 = (bf16[256,1024]{0,1:T(8,128)(2,1)S(1)}, bf16[256,1024]{0,1:T(8,128)(2,1)S(1)}, u32[]{:S(2)}, u32[]{:S(2)}) collective-permute-start(bf16[256,1024]{0,1:T(8,128)(2,1)S(1)} %bitcast.134), channel_id=1, source_target_pairs={{6,0},{8,2},{10,4},{12,6},{14,8},{16,10},{18,12},{20,14},{22,16},{... | collective-permute-start | bytes 1572872 | tf_op jit(solution)/shard_map/ppermute | solution.py:21
  123.3 2.1 collective-permute-start.16
  125.4 7.5 %collective-permute-done.18 = bf16[256,1024]{0,1:T(8,128)(2,1)S(1)} collective-permute-done((bf16[256,1024]{0,1:T(8,128)(2,1)S(1)}, bf16[256,1024]{0,1:T(8,128)(2,1)S(1)}, u32[]{:S(2)}, u32[]{:S(2)}) %collective-permute-start.18) | collective-permute-done | bytes 524320 | tf_op jit(solution)/shard_map/ppermute | solution.py:21
  132.9 11.2 %collective-permute-done.17 = bf16[256,1024]{0,1:T(8,128)(2,1)S(1)} collective-permute-done((bf16[256,1024]{0,1:T(8,128)(2,1)S(1)}, bf16[256,1024]{0,1:T(8,128)(2,1)S(1)}, u32[]{:S(2)}, u32[]{:S(2)}) %collective-permute-start.17) | collective-permute-done | bytes 524320 | tf_op jit(solution)/shard_map/ppermute | solution.py:21
  144.2 2.0 collective-permute-done.16
  146.6 9.0 %convolution_bitcast_fusion = f32[5376,1024]{0,1:T(8,128)} fusion(bf16[256,1024]{0,1:T(8,128)(2,1)S(1)} %fusion.37, bf16[1,256,5376]{2,1,0:T(8,128)(2,1)S(1)} %copy-done), kind=kOutput, calls=%fused_computation.8 | convolution fusion | flops 2818572288 | bytes 25296896 | tf_op jit(solution)/shard_map/dot_general | solution.py:112
  155.6 21.7 %copy.99 = f32[5376,1024]{1,0:T(8,128)} copy(f32[5376,1024]{0,1:T(8,128)} %convolution_bitcast_fusion) | data formatting | bytes 44040192
  177.4 7.3 %fusion.31 = bf16[256,1024]{1,0:T(8,128)(2,1)S(1)} fusion(bf16[5376,1024]{1,0:T(8,128)(2,1)} %all-gather.2.cloned.1.call-done, bf16[1,256,5376]{2,1,0:T(8,128)(2,1)S(1)} %copy-done), kind=kOutput, calls=%fused_computation.36 | convolution fusion | flops 2818834432 | bytes 14286848 | tf_op jit(solution)/shard_map/dot_general | solution.py:35
  184.7 2.1 collective-permute-start.3
  186.7 4.8 %collective-permute-start.2 = (bf16[256,1024]{1,0:T(8,128)(2,1)S(1)}, bf16[256,1024]{1,0:T(8,128)(2,1)S(1)}, u32[]{:S(2)}, u32[]{:S(2)}) collective-permute-start(bf16[256,1024]{1,0:T(8,128)(2,1)S(1)} %fusion.31), channel_id=1, source_target_pairs={{0,4},{2,6},{4,8},{6,10},{8,12},{10,14},{12,16},{14,18},{16,20},{1... | collective-permute-start | bytes 1572872 | tf_op jit(solution)/shard_map/ppermute | solution.py:21
  191.5 4.3 collective-permute-start.1
  197.7 13.7 %fusion.4 = bf16[1,256,5376]{2,1,0:T(8,128)(2,1)} fusion(bf16[256,1024]{0,1:T(8,128)(2,1)S(1)} %fusion.37, bf16[5376,1024]{1,0:T(8,128)(2,1)} %all-gather.2.cloned.1.call-done), kind=kOutput, calls=%fused_computation.10 | convolution fusion | flops 2819948544 | bytes 14286848 | tf_op jit(solution)/shard_map/dot_general | solution.py:108
  213.3 2.1 collective-permute-done.1
  217.0 2.7 multiply_reduce_fusion
  219.7 14.8 %fusion.3 = bf16[8,2,256,1280]{2,3,1,0:T(8,128)(2,1)} fusion(bf16[256,8,2,128]{0,3,2,1:T(8,128)(2,1)S(1)} %bitcast.117, f32[8,2,256]{2,1,0:T(2,128)S(1)} %bitcast.136, f32[8,2,256]{2,1,0:T(2,128)S(1)} %get-tuple-element.30, f32[8,2,256,1280]{2,3,1,0:T(8,128)} %get-tuple-element.31, bf16[1280,8,128,1]{2,1,0,3:T(8,128)(2,1)S(1)} %bitcast.114), kind=kOutput, calls=%fused_computation.4 | convolution fusion | flops 1363148800 | bytes 35160064 | tf_op jit(solution)/shard_map/tgrd,lgd->grtl/dot_general | solution.py:66
  234.5 7.7 %fusion.8 = bf16[1280,8,128]{0,2,1:T(8,128)(2,1)S(1)} fusion(bf16[8,2,256,1280]{2,3,1,0:T(8,128)(2,1)} %fusion.3, bf16[256,8,2,128]{0,3,2,1:T(8,128)(2,1)} %bitcast.131), kind=kOutput, calls=%fused_computation.16 | convolution fusion | flops 1344798720 | bytes 14155776 | tf_op jit(solution)/shard_map/grtl,tgrd->lgd/dot_general | solution.py:79
  243.7 2.1 copy.73
  245.8 2.0 copy.77
  247.9 2.0 copy.76
  250.9 11.5 %collective-permute-start.13 = (bf16[256,1024]{1,0:T(8,128)(2,1)}, bf16[256,1024]{1,0:T(8,128)(2,1)}, u32[]{:S(2)}, u32[]{:S(2)}) collective-permute-start(bf16[256,1024]{1,0:T(8,128)(2,1)} %copy.75), channel_id=1, source_target_pairs={{4,0},{6,2},{8,4},{10,6},{12,8},{14,10},{16,12},{18,14},{20,16},{2... | collective-permute-start | bytes 1572872 | tf_op jit(solution)/shard_map/ppermute | solution.py:21
  266.3 2.1 collective-permute-start.12
  268.5 6.8 %multiply_convert_fusion = bf16[8,128,2,256]{3,1,2,0:T(8,128)(2,1)S(1)} fusion(bf16[8,2,256,1280]{2,3,1,0:T(8,128)(2,1)} %fusion.3, bf16[1280,8,128]{2,0,1:T(8,128)(2,1)} %constant_dynamic-update-slice_fusion.5), kind=kOutput, calls=%fused_computation.28 | convolution fusion | flops 1343225856 | bytes 14155776 | tf_op jit(solution)/shard_map/grtl,lgd->tgrd/dot_general | solution.py:74
  279.2 2.7 copy.74
  281.9 15.4 %collective-permute-done.13 = bf16[256,1024]{1,0:T(8,128)(2,1)} collective-permute-done((bf16[256,1024]{1,0:T(8,128)(2,1)}, bf16[256,1024]{1,0:T(8,128)(2,1)}, u32[]{:S(2)}, u32[]{:S(2)}) %collective-permute-start.13) | collective-permute-done | bytes 524320 | tf_op jit(solution)/shard_map/ppermute | solution.py:21
  297.3 24.4 %collective-permute-done.14 = bf16[256,1024]{1,0:T(8,128)(2,1)} collective-permute-done((bf16[256,1024]{1,0:T(8,128)(2,1)}, bf16[256,1024]{1,0:T(8,128)(2,1)}, u32[]{:S(2)}, u32[]{:S(2)}) %collective-permute-start.14) | collective-permute-done | bytes 524320 | tf_op jit(solution)/shard_map/ppermute | solution.py:21
  321.7 13.3 %collective-permute-done.15 = bf16[256,1024]{1,0:T(8,128)(2,1)} collective-permute-done((bf16[256,1024]{1,0:T(8,128)(2,1)}, bf16[256,1024]{1,0:T(8,128)(2,1)}, u32[]{:S(2)}, u32[]{:S(2)}) %collective-permute-start.15) | collective-permute-done | bytes 524320 | tf_op jit(solution)/shard_map/ppermute | solution.py:21
  335.0 3.2 fusion.38
  338.2 100.2 %reduce-scatter.4.cloned.1.call-done = f32[168,1024]{1,0:T(8,128)} async-done(((f32[5376,1024]{1,0:T(8,128)}), f32[168,1024]{1,0:T(8,128)}) %reduce-scatter.4.cloned.1.call-update) | async-done | bytes 688144
  (78 shorter events, 33.3 us)
Async XLA Ops:
  8.0 138.6 %copy-start = (bf16[1,256,5376]{2,1,0:T(8,128)(2,1)S(1)}, bf16[1,256,5376]{2,1,0:T(8,128)(2,1)}, u32[]{:S(2)}) copy-start(bf16[1,256,5376]{2,1,0:T(8,128)(2,1)} %param.6) | copy-start | bytes 8257540
  8.0 169.3 %all-gather.2.cloned.1.call-start = ((), (), s32[]{:S(2)}) async-start(), calls=%async_computation.1 | async-start | bytes 16515072 | tf_op jit(solution)/shard_map/all_gather | solution.py:34
  8.9 17.2 %copy-start.8 = (s32[1,256]{1,0:T(1,128)S(1)}, s32[1,256]{1,0:T(1,128)}, u32[]{:S(2)}) copy-start(s32[1,256]{1,0:T(1,128)} %param.11) | copy-start | bytes 3076
  8.9 30.5 %collective-permute-start.7 = (bf16[256]{0:T(256)(128)(2,1)S(1)}, bf16[256]{0:T(256)(128)(2,1)S(1)}, u32[]{:S(2)}, u32[]{:S(2)}) collective-permute-start(bf16[256]{0:T(256)(128)(2,1)S(1)} %convert_reduce_fusion), channel_id=1, source_target_pairs={{0,2},{2,4},{4,6},{6,8},{8,10},{10,12},{12,14},{14,16},{16,18},{18... | collective-permute-start | bytes 1544 | tf_op jit(solution)/shard_map/ppermute | solution.py:21
  12.8 24.5 %collective-permute-start.6 = (bf16[256]{0:T(256)(128)(2,1)S(1)}, bf16[256]{0:T(256)(128)(2,1)S(1)}, u32[]{:S(2)}, u32[]{:S(2)}) collective-permute-start(bf16[256]{0:T(256)(128)(2,1)S(1)} %convert_reduce_fusion), channel_id=1, source_target_pairs={{0,4},{2,6},{4,8},{6,10},{8,12},{10,14},{12,16},{14,18},{16,20},{1... | collective-permute-start | bytes 1544 | tf_op jit(solution)/shard_map/ppermute | solution.py:21
  15.9 19.2 %collective-permute-start.5 = (bf16[256]{0:T(256)(128)(2,1)S(1)}, bf16[256]{0:T(256)(128)(2,1)S(1)}, u32[]{:S(2)}, u32[]{:S(2)}) collective-permute-start(bf16[256]{0:T(256)(128)(2,1)S(1)} %convert_reduce_fusion), channel_id=1, source_target_pairs={{0,6},{2,8},{4,10},{6,12},{8,14},{10,16},{12,18},{14,20},{16,22},{... | collective-permute-start | bytes 1544 | tf_op jit(solution)/shard_map/ppermute | solution.py:21
  18.2 13.9 %collective-permute-start.4 = (bf16[256]{0:T(256)(128)(2,1)S(1)}, bf16[256]{0:T(256)(128)(2,1)S(1)}, u32[]{:S(2)}, u32[]{:S(2)}) collective-permute-start(bf16[256]{0:T(256)(128)(2,1)S(1)} %convert_reduce_fusion), channel_id=1, source_target_pairs={{0,8},{2,10},{4,12},{6,14},{8,16},{10,18},{12,20},{14,22},{16,24},... | collective-permute-start | bytes 1544 | tf_op jit(solution)/shard_map/ppermute | solution.py:21
  21.4 417.0 %reduce-scatter.4.cloned.1.call-start = ((), (), s32[]{:S(2)}) async-start(), calls=%async_computation.2 | async-start | bytes 22708224
  22.7 18.7 %collective-permute-start.11 = (bf16[256,1024]{0,1:T(8,128)(2,1)S(1)}, bf16[256,1024]{0,1:T(8,128)(2,1)}, u32[]{:S(2)}, u32[]{:S(2)}) collective-permute-start(bf16[256,1024]{0,1:T(8,128)(2,1)S(1)} %bitcast.125), channel_id=1, source_target_pairs={{0,2},{2,4},{4,6},{6,8},{8,10},{10,12},{12,14},{14,16},{16,18},{18... | collective-permute-start | bytes 1572872 | tf_op jit(solution)/shard_map/ppermute | solution.py:21
  32.0 16.4 %collective-permute-start.10 = (bf16[256,1024]{0,1:T(8,128)(2,1)S(1)}, bf16[256,1024]{0,1:T(8,128)(2,1)}, u32[]{:S(2)}, u32[]{:S(2)}) collective-permute-start(bf16[256,1024]{0,1:T(8,128)(2,1)S(1)} %bitcast.127), channel_id=1, source_target_pairs={{0,4},{2,6},{4,8},{6,10},{8,12},{10,14},{12,16},{14,18},{16,20},{1... | collective-permute-start | bytes 1572872 | tf_op jit(solution)/shard_map/ppermute | solution.py:21
  35.1 25.2 %collective-permute-start.9 = (bf16[256,1024]{0,1:T(8,128)(2,1)S(1)}, bf16[256,1024]{0,1:T(8,128)(2,1)}, u32[]{:S(2)}, u32[]{:S(2)}) collective-permute-start(bf16[256,1024]{0,1:T(8,128)(2,1)S(1)} %bitcast.128), channel_id=1, source_target_pairs={{0,6},{2,8},{4,10},{6,12},{8,14},{10,16},{12,18},{14,20},{16,22},{... | collective-permute-start | bytes 1572872 | tf_op jit(solution)/shard_map/ppermute | solution.py:21
  37.2 25.1 %collective-permute-start.8 = (bf16[256,1024]{0,1:T(8,128)(2,1)S(1)}, bf16[256,1024]{0,1:T(8,128)(2,1)}, u32[]{:S(2)}, u32[]{:S(2)}) collective-permute-start(bf16[256,1024]{0,1:T(8,128)(2,1)S(1)} %bitcast.129), channel_id=1, source_target_pairs={{0,8},{2,10},{4,12},{6,14},{8,16},{10,18},{12,20},{14,22},{16,24},... | collective-permute-start | bytes 1572872 | tf_op jit(solution)/shard_map/ppermute | solution.py:21
  62.4 8.9 %copy-start.6 = (bf16[256,8,128]{2,0,1:T(8,128)(2,1)S(1)}, bf16[256,8,128]{2,0,1:T(8,128)(2,1)}, u32[]{:S(2)}) copy-start(bf16[256,8,128]{2,0,1:T(8,128)(2,1)} %copy.62) | copy-start | bytes 1572868
  64.5 5.9 %copy-start.7 = (bf16[256,8,128]{2,0,1:T(8,128)(2,1)S(1)}, bf16[256,8,128]{2,0,1:T(8,128)(2,1)}, u32[]{:S(2)}) copy-start(bf16[256,8,128]{2,0,1:T(8,128)(2,1)} %copy.61) | copy-start | bytes 1572868
  84.5 14.4 %copy-start.2 = (bf16[1,256,2048]{1,2,0:T(8,128)(2,1)S(1)}, bf16[1,256,2048]{1,2,0:T(8,128)(2,1)}, u32[]{:S(2)}) copy-start(bf16[1,256,2048]{1,2,0:T(8,128)(2,1)} %copy.66) | copy-start | bytes 3145732
  109.7 15.7 %collective-permute-start.19 = (bf16[256,1024]{0,1:T(8,128)(2,1)S(1)}, bf16[256,1024]{0,1:T(8,128)(2,1)S(1)}, u32[]{:S(2)}, u32[]{:S(2)}) collective-permute-start(bf16[256,1024]{0,1:T(8,128)(2,1)S(1)} %bitcast.135), channel_id=1, source_target_pairs={{8,0},{10,2},{12,4},{14,6},{16,8},{18,10},{20,12},{22,14},{24,16},... | collective-permute-start | bytes 1572872 | tf_op jit(solution)/shard_map/ppermute | solution.py:21
  111.6 21.3 %collective-permute-start.18 = (bf16[256,1024]{0,1:T(8,128)(2,1)S(1)}, bf16[256,1024]{0,1:T(8,128)(2,1)S(1)}, u32[]{:S(2)}, u32[]{:S(2)}) collective-permute-start(bf16[256,1024]{0,1:T(8,128)(2,1)S(1)} %bitcast.134), channel_id=1, source_target_pairs={{6,0},{8,2},{10,4},{12,6},{14,8},{16,10},{18,12},{20,14},{22,16},{... | collective-permute-start | bytes 1572872 | tf_op jit(solution)/shard_map/ppermute | solution.py:21
  121.4 22.8 %collective-permute-start.17 = (bf16[256,1024]{0,1:T(8,128)(2,1)S(1)}, bf16[256,1024]{0,1:T(8,128)(2,1)S(1)}, u32[]{:S(2)}, u32[]{:S(2)}) collective-permute-start(bf16[256,1024]{0,1:T(8,128)(2,1)S(1)} %bitcast.133), channel_id=1, source_target_pairs={{4,0},{6,2},{8,4},{10,6},{12,8},{14,10},{16,12},{18,14},{20,16},{2... | collective-permute-start | bytes 1572872 | tf_op jit(solution)/shard_map/ppermute | solution.py:21
  123.3 22.9 %collective-permute-start.16 = (bf16[256,1024]{0,1:T(8,128)(2,1)S(1)}, bf16[256,1024]{0,1:T(8,128)(2,1)S(1)}, u32[]{:S(2)}, u32[]{:S(2)}) collective-permute-start(bf16[256,1024]{0,1:T(8,128)(2,1)S(1)} %bitcast.132), channel_id=1, source_target_pairs={{2,0},{4,2},{6,4},{8,6},{10,8},{12,10},{14,12},{16,14},{18,16},{20... | collective-permute-start | bytes 1572872 | tf_op jit(solution)/shard_map/ppermute | solution.py:21
  177.3 38.9 %slice-start = ((s8[10485760]{0:T(1024)(128)(4,1)}), s8[4194304]{0:T(1024)(128)(4,1)S(1)}, s32[]{:S(2)}) async-start(s8[10485760]{0:T(1024)(128)(4,1)} %bitcast.111), calls=%async_computation.3 | async-start | bytes 8388608
  177.3 38.9 %slice-start.1 = ((s8[10485760]{0:T(1024)(128)(4,1)}), s8[4194304]{0:T(1024)(128)(4,1)S(1)}, s32[]{:S(2)}) async-start(s8[10485760]{0:T(1024)(128)(4,1)} %bitcast.111), calls=%async_computation.4 | async-start | bytes 8388608
  184.6 31.7 %slice-start.2 = ((s8[10485760]{0:T(1024)(128)(4,1)}), s8[2097152]{0:T(1024)(128)(4,1)S(1)}, s32[]{:S(2)}) async-start(s8[10485760]{0:T(1024)(128)(4,1)} %bitcast.111), calls=%async_computation.5 | async-start | bytes 4194304
  184.7 30.9 %collective-permute-start.3 = (bf16[256,1024]{1,0:T(8,128)(2,1)S(1)}, bf16[256,1024]{1,0:T(8,128)(2,1)S(1)}, u32[]{:S(2)}, u32[]{:S(2)}) collective-permute-start(bf16[256,1024]{1,0:T(8,128)(2,1)S(1)} %fusion.31), channel_id=1, source_target_pairs={{0,2},{2,4},{4,6},{6,8},{8,10},{10,12},{12,14},{14,16},{16,18},{18... | collective-permute-start | bytes 1572872 | tf_op jit(solution)/shard_map/ppermute | solution.py:21
  186.7 28.7 %collective-permute-start.2 = (bf16[256,1024]{1,0:T(8,128)(2,1)S(1)}, bf16[256,1024]{1,0:T(8,128)(2,1)S(1)}, u32[]{:S(2)}, u32[]{:S(2)}) collective-permute-start(bf16[256,1024]{1,0:T(8,128)(2,1)S(1)} %fusion.31), channel_id=1, source_target_pairs={{0,4},{2,6},{4,8},{6,10},{8,12},{10,14},{12,16},{14,18},{16,20},{1... | collective-permute-start | bytes 1572872 | tf_op jit(solution)/shard_map/ppermute | solution.py:21
  191.5 23.9 %collective-permute-start.1 = (bf16[256,1024]{1,0:T(8,128)(2,1)S(1)}, bf16[256,1024]{1,0:T(8,128)(2,1)S(1)}, u32[]{:S(2)}, u32[]{:S(2)}) collective-permute-start(bf16[256,1024]{1,0:T(8,128)(2,1)S(1)} %fusion.31), channel_id=1, source_target_pairs={{0,6},{2,8},{4,10},{6,12},{8,14},{10,16},{12,18},{14,20},{16,22},{... | collective-permute-start | bytes 1572872 | tf_op jit(solution)/shard_map/ppermute | solution.py:21
  195.8 17.5 %collective-permute-start = (bf16[256,1024]{1,0:T(8,128)(2,1)S(1)}, bf16[256,1024]{1,0:T(8,128)(2,1)S(1)}, u32[]{:S(2)}, u32[]{:S(2)}) collective-permute-start(bf16[256,1024]{1,0:T(8,128)(2,1)S(1)} %fusion.31), channel_id=1, source_target_pairs={{0,8},{2,10},{4,12},{6,14},{8,16},{10,18},{12,20},{14,22},{16,24},... | collective-permute-start | bytes 1572872 | tf_op jit(solution)/shard_map/ppermute | solution.py:21
  215.6 1.4 copy-start.3
  243.7 6.2 %copy-start.5 = (bf16[256,8,128]{0,2,1:T(8,128)(2,1)S(1)}, bf16[256,8,128]{0,2,1:T(8,128)(2,1)}, u32[]{:S(2)}) copy-start(bf16[256,8,128]{0,2,1:T(8,128)(2,1)} %get-tuple-element.28) | copy-start | bytes 1572868
  250.9 46.4 %collective-permute-start.13 = (bf16[256,1024]{1,0:T(8,128)(2,1)}, bf16[256,1024]{1,0:T(8,128)(2,1)}, u32[]{:S(2)}, u32[]{:S(2)}) collective-permute-start(bf16[256,1024]{1,0:T(8,128)(2,1)} %copy.75), channel_id=1, source_target_pairs={{4,0},{6,2},{8,4},{10,6},{12,8},{14,10},{16,12},{18,14},{20,16},{2... | collective-permute-start | bytes 1572872 | tf_op jit(solution)/shard_map/ppermute | solution.py:21
  262.5 59.2 %collective-permute-start.14 = (bf16[256,1024]{1,0:T(8,128)(2,1)}, bf16[256,1024]{1,0:T(8,128)(2,1)}, u32[]{:S(2)}, u32[]{:S(2)}) collective-permute-start(bf16[256,1024]{1,0:T(8,128)(2,1)} %copy.76), channel_id=1, source_target_pairs={{6,0},{8,2},{10,4},{12,6},{14,8},{16,10},{18,12},{20,14},{22,16},{... | collective-permute-start | bytes 1572872 | tf_op jit(solution)/shard_map/ppermute | solution.py:21
  264.4 70.5 %collective-permute-start.15 = (bf16[256,1024]{1,0:T(8,128)(2,1)}, bf16[256,1024]{1,0:T(8,128)(2,1)}, u32[]{:S(2)}, u32[]{:S(2)}) collective-permute-start(bf16[256,1024]{1,0:T(8,128)(2,1)} %copy.77), channel_id=1, source_target_pairs={{8,0},{10,2},{12,4},{14,6},{16,8},{18,10},{20,12},{22,14},{24,16},... | collective-permute-start | bytes 1572872 | tf_op jit(solution)/shard_map/ppermute | solution.py:21
  266.3 68.6 %collective-permute-start.12 = (bf16[256,1024]{1,0:T(8,128)(2,1)}, bf16[256,1024]{1,0:T(8,128)(2,1)}, u32[]{:S(2)}, u32[]{:S(2)}) collective-permute-start(bf16[256,1024]{1,0:T(8,128)(2,1)} %copy.73), channel_id=1, source_target_pairs={{2,0},{4,2},{6,4},{8,6},{10,8},{12,10},{14,12},{16,14},{18,16},{20... | collective-permute-start | bytes 1572872 | tf_op jit(solution)/shard_map/ppermute | solution.py:21
  275.3 1.4 copy-start.4
  278.1 160.3 %copy-start.1 = (bf16[1,256,5376]{2,1,0:T(8,128)(2,1)S(1)}, bf16[1,256,5376]{2,1,0:T(8,128)(2,1)}, u32[]{:S(2)}) copy-start(bf16[1,256,5376]{2,1,0:T(8,128)(2,1)} %param.6) | copy-start | bytes 8257540
Sparse Core Ops, SparseCore 0:
  21.5 134.3 all-gather.1
Sparse Core Ops, SparseCore 1:
  177.4 260.9 reduce-scatter.3
where the time goes:
time: 450 us; the launch traced here: 446 us
  waiting for transfers between devices  193 us (43%)
  matrix products  83.2 us (18%)
  starting transfers between devices  68.7 us (15%)
  local copies, waits for them, and re-layouts  63.4 us (14%)
  other arithmetic  21.7 us (5%)
  between operations  15.9 us (4%)
    unnamed x3, waiting for transfers between devices  100 us
    ppermute x20, waiting for transfers between devices, shifted(): return lax.ppermute(x, axis, pairs)  92.6 us
    ppermute x20, starting transfers between devices, shifted(): return lax.ppermute(x, axis, pairs)  68.7 us
    unnamed x42, local copies, waits for them, and re-layouts  37.6 us
    dot_general x1, matrix products, shards(): jnp.einsum('tgrd,lgd->grtl', grad_heads, window_values, preferred_element...  14.8 us
    convert_element_type x1, other arithmetic, shards(): probs_low = probs.astype(jnp.bfloat16)  14.4 us
    dot_general x1, matrix products, shards(): lax.dot_general(d_values_low, w_full, (((1,), (1,)), ((), ())), preferred...  13.7 us
    sub x1, matrix products, shards(): raw_weights = jnp.exp(scores - highest)  12.2 us
  transfers between devices with their start and end apart: 22, of which 11 were waited for; matrix products, arithmetic and copies ran while one was open for 37% of the time, Pallas kernels for 0%

commit v1 on v0

v1 whole, which is shorter than its diff:
```python
import functools
import math

import jax
import jax.numpy as jnp
from jax import lax
from jax.experimental import pallas as pl
from jax.experimental.pallas import tpu as pltpu
from jax.sharding import PartitionSpec as P

HQ = 16
HK = 8
HD = 128
WINDOW = 1024
GROUP = 2
NEG = -1e30

score_scale = 1.0 / math.sqrt(168.0)
exp2_scale = score_scale / math.log(2.0)

BF16 = jnp.bfloat16
F32 = jnp.float32
NT = (((1,), (1,)), ((), ()))
TN = (((0,), (0,)), ((), ()))


def dot(a, b, dims=(((1,), (0,)), ((), ()))):
    return lax.dot_general(a, b, dims, preferred_element_type=F32)


def stacked(ref, rows):
    return jnp.concatenate([ref[rows, r * HD : (r + 1) * HD] for r in range(GROUP)], 0)


def probs_kernel(blk, n_back, low_ref, q_ref, do_ref, *refs):
    n_arr = n_back + 1
    k_refs = refs[:n_arr]
    e_ref, inv_ref, dot_ref = refs[n_arr : n_arr + 3]
    dv_refs = refs[n_arr + 3 : 2 * n_arr + 3]
    bias, s_scr, dv_acc = refs[2 * n_arr + 3 :]
    span_blocks = WINDOW // blk + 1

    @pl.when(pl.program_id(0) == 0)
    def _():
        for qb in range(2):
            kpos = lax.broadcasted_iota(jnp.int32, (span_blocks * blk, blk), 0) + qb * blk
            qpos = lax.broadcasted_iota(jnp.int32, (span_blocks * blk, blk), 1) + (qb * blk + WINDOW)
            low = low_ref[:, qb * blk : (qb + 1) * blk]
            ok = (kpos >= low) & (kpos <= qpos)
            bias[qb] = jnp.where(ok, 0.0, NEG)

    def key_block(j):
        return k_refs[j // 2][(j % 2) * blk : (j % 2 + 1) * blk, :]

    for qb in range(2):
        rows = slice(qb * blk, (qb + 1) * blk)
        qs = stacked(q_ref, rows)
        top = None
        for j in range(span_blocks):
            s = dot(key_block(qb + j), qs, NT)
            b = bias[qb, j * blk : (j + 1) * blk, :]
            s = s * exp2_scale + jnp.concatenate([b] * GROUP, 1)
            s_scr[j] = s
            part = jnp.max(s.reshape(blk // 8, 8, GROUP * blk), axis=0)
            top = part if top is None else jnp.maximum(top, part)
        top = jnp.max(top, axis=0, keepdims=True)
        total = None
        for j in range(span_blocks):
            e = jnp.exp2(s_scr[j] - top)
            part = jnp.sum(e.reshape(blk // 8, 8, GROUP * blk), axis=0)
            total = part if total is None else total + part
            e_ref[0, qb, j * blk : (j + 1) * blk, :] = e.astype(BF16)
        inv = 1.0 / jnp.sum(total, axis=0, keepdims=True)
        inv_ref[0, qb] = inv
        do_t = (stacked(do_ref, rows).astype(F32).T * inv).astype(BF16)
        dot_ref[0, qb] = do_t
        for j in range(span_blocks):
            term = dot(e_ref[0, qb, j * blk : (j + 1) * blk, :], do_t, NT)
            at = slice((qb + j) * blk, (qb + j + 1) * blk)
            if qb == 0 or j == span_blocks - 1:
                dv_acc[at, :] = term
            else:
                dv_acc[at, :] += term
    for a in range(n_arr):
        dv_refs[a][...] = dv_acc[a * 2 * blk : (a + 1) * 2 * blk, :].astype(BF16)


def grads_kernel(blk, n_back, e_ref, inv_ref, dot_ref, q_ref, *refs):
    n_arr = n_back + 1
    k_refs = refs[:n_arr]
    v_refs = refs[n_arr : 2 * n_arr]
    out_ref, dq_ref = refs[2 * n_arr : 2 * n_arr + 2]
    dk_refs = refs[2 * n_arr + 2 : 3 * n_arr + 2]
    (dk_acc,) = refs[3 * n_arr + 2 :]
    span_blocks = WINDOW // blk + 1

    def block_of(arrays, j):
        return arrays[j // 2][(j % 2) * blk : (j % 2 + 1) * blk, :]

    for qb in range(2):
        rows = slice(qb * blk, (qb + 1) * blk)
        qs = stacked(q_ref, rows)
        do_t = dot_ref[0, qb]
        out_t = None
        for j in range(span_blocks):
            e = e_ref[0, qb, j * blk : (j + 1) * blk, :]
            part = dot(block_of(v_refs, qb + j), e, TN)
            out_t = part if out_t is None else out_t + part
        out_t = (out_t * inv_ref[0, qb]).astype(BF16).astype(F32)
        delta = jnp.sum(out_t * do_t.astype(F32), axis=0, keepdims=True)
        out = out_t.T.astype(BF16)
        dq_t = None
        for j in range(span_blocks):
            e = e_ref[0, qb, j * blk : (j + 1) * blk, :].astype(F32)
            dp = dot(block_of(v_refs, qb + j), do_t)
            ds = (e * (dp - delta)).astype(BF16)
            term = dot(ds, qs)
            at = slice((qb + j) * blk, (qb + j + 1) * blk)
            if qb == 0 or j == span_blocks - 1:
                dk_acc[at, :] = term
            else:
                dk_acc[at, :] += term
            part = dot(block_of(k_refs, qb + j), ds, TN)
            dq_t = part if dq_t is None else dq_t + part
        dq = (dq_t * score_scale).T.astype(BF16)
        for r in range(GROUP):
            out_ref[rows, r * HD : (r + 1) * HD] = out[r * blk : (r + 1) * blk, :]
            dq_ref[rows, r * HD : (r + 1) * HD] = dq[r * blk : (r + 1) * blk, :]
    for a in range(n_arr):
        dk_refs[a][...] = (dk_acc[a * 2 * blk : (a + 1) * 2 * blk, :] * score_scale).astype(BF16)


def run_probs(low, q, do, keys):
    rows, width = keys[0].shape
    blk = rows // 2
    heads = width // HD
    n_arr = len(keys)
    span = WINDOW + blk
    lanes = GROUP * blk
    head_block = pl.BlockSpec((rows, HD), lambda g: (0, g))
    group_block = pl.BlockSpec((rows, GROUP * HD), lambda g: (0, g))
    return pl.pallas_call(
        functools.partial(probs_kernel, blk, n_arr - 1),
        grid=(heads,),
        in_specs=[pl.BlockSpec((1, rows), lambda g: (0, 0)), group_block, group_block] + [head_block] * n_arr,
        out_specs=[
            pl.BlockSpec((1, 2, span, lanes), lambda g: (g, 0, 0, 0)),
            pl.BlockSpec((1, 2, 1, lanes), lambda g: (g, 0, 0, 0)),
            pl.BlockSpec((1, 2, HD, lanes), lambda g: (g, 0, 0, 0)),
        ]
        + [head_block] * n_arr,
        out_shape=[
            jax.ShapeDtypeStruct((heads, 2, span, lanes), BF16),
            jax.ShapeDtypeStruct((heads, 2, 1, lanes), F32),
            jax.ShapeDtypeStruct((heads, 2, HD, lanes), BF16),
        ]
        + [jax.ShapeDtypeStruct((rows, width), BF16)] * n_arr,
        scratch_shapes=[
            pltpu.VMEM((2, span, blk), F32),
            pltpu.VMEM((span // blk, blk, lanes), F32),
            pltpu.VMEM((WINDOW + rows, HD), F32),
        ],
        compiler_params=pltpu.CompilerParams(vmem_limit_bytes=40 * 1024 * 1024),
        cost_estimate=pl.CostEstimate(
            flops=heads * 2 * span * lanes * HD * 2 * 2 * 6,
            bytes_accessed=heads * 2 * span * lanes * 2,
            transcendentals=0,
        ),
        name="probs",
    )(low, q, do, *keys)


def run_grads(e, inv, do_t, q, keys, values):
    rows, width = keys[0].shape
    blk = rows // 2
    heads = width // HD
    n_arr = len(keys)
    span = WINDOW + blk
    lanes = GROUP * blk
    head_block = pl.BlockSpec((rows, HD), lambda g: (0, g))
    group_block = pl.BlockSpec((rows, GROUP * HD), lambda g: (0, g))
    return pl.pallas_call(
        functools.partial(grads_kernel, blk, n_arr - 1),
        grid=(heads,),
        in_specs=[
            pl.BlockSpec((1, 2, span, lanes), lambda g: (g, 0, 0, 0)),
            pl.BlockSpec((1, 2, 1, lanes), lambda g: (g, 0, 0, 0)),
            pl.BlockSpec((1, 2, HD, lanes), lambda g: (g, 0, 0, 0)),
            group_block,
        ]
        + [head_block] * (2 * n_arr),
        out_specs=[group_block, group_block] + [head_block] * n_arr,
        out_shape=[jax.ShapeDtypeStruct((rows, GROUP * width), BF16)] * 2
        + [jax.ShapeDtypeStruct((rows, width), BF16)] * n_arr,
        scratch_shapes=[pltpu.VMEM((WINDOW + rows, HD), F32)],
        compiler_params=pltpu.CompilerParams(vmem_limit_bytes=40 * 1024 * 1024),
        cost_estimate=pl.CostEstimate(
            flops=heads * 2 * span * lanes * HD * 2 * 4 * 4,
            bytes_accessed=heads * 2 * span * lanes * 2,
            transcendentals=0,
        ),
        name="grads",
    )(e, inv, do_t, q, *keys, *values)


def shifted(x, axis, by):
    length = lax.axis_size(axis)
    return lax.ppermute(x, axis, [(i, i + by) for i in range(length) if 0 <= i + by < length])


def swapped(x):
    return lax.ppermute(x, "ctx", [(i, i ^ 1) for i in range(lax.axis_size("ctx"))])


def rotated(x, axis, by):
    length = lax.axis_size(axis)
    return lax.ppermute(x, axis, [(i, (i + by) % length) for i in range(length)])


def cols(x, at, width):
    return lax.dynamic_slice_in_dim(x, at * width, width, x.ndim - 1)


def pair(core, own, other, axis):
    return jnp.where(core == 0, jnp.concatenate([own, other], axis), jnp.concatenate([other, own], axis))


def to_heads(core, x):
    half = x.shape[1] // 2
    return pair(core, cols(x, core, half), swapped(cols(x, 1 - core, half)), 0)


def to_tokens(core, x):
    half = x.shape[0] // 2
    own = lax.dynamic_slice_in_dim(x, core * half, half, 0)
    other = swapped(lax.dynamic_slice_in_dim(x, (1 - core) * half, half, 0))
    return pair(core, own, other, 1)


def shards(hidden, queries, key_heads, w_value, d_out, segments):
    shard_rows = hidden.shape[1]
    model = hidden.shape[2]
    kv_width = w_value.shape[1]
    n_ctx = lax.axis_size("ctx")
    n_fsdp = lax.axis_size("fsdp")
    chip_rows = 2 * shard_rows
    n_back = WINDOW // chip_rows
    my_ctx = lax.axis_index("ctx")
    my_fsdp = lax.axis_index("fsdp")
    core = my_ctx % 2
    chip = my_ctx // 2
    half_kv = kv_width // 2
    slab = model // n_fsdp
    tokens = hidden[0]

    k_own = to_heads(core, key_heads[0])
    keys = [shifted(k_own, "ctx", 2 * d) for d in range(n_back, 0, -1)] + [k_own]
    q_chip = to_heads(core, queries[0])
    do_chip = to_heads(core, d_out[0])

    slabs = [cols(tokens, my_fsdp, slab)]
    for s in range(1, n_fsdp):
        slabs.append(rotated(cols(tokens, (my_fsdp + s) % n_fsdp, slab), "fsdp", s))
    value_sum = dot(slabs[0], w_value)
    for s in range(1, n_fsdp):
        back = rotated(dot(slabs[s], w_value).astype(BF16), "fsdp", -s)
        value_sum = value_sum + back.astype(F32)
    v_own = to_heads(core, value_sum.astype(BF16))
    vals = [shifted(v_own, "ctx", 2 * d) for d in range(n_back, 0, -1)] + [v_own]

    tags = lax.all_gather(segments[0], "ctx", axis=0, tiled=True)
    chip_tags = lax.dynamic_slice_in_dim(tags, chip * chip_rows, chip_rows, 0)
    doc_start = jnp.sum((tags[None, :] < chip_tags[:, None]).astype(jnp.int32), axis=1)
    first = chip * chip_rows
    q_pos = first + jnp.arange(chip_rows, dtype=jnp.int32)
    low = (jnp.maximum(doc_start, q_pos - (WINDOW - 1)) - (first - WINDOW))[None, :]

    e, inv, do_t, *dv_terms = run_probs(low, q_chip, do_chip, keys)
    dv_total = dv_terms[n_back].astype(F32)
    for d in range(1, n_back + 1):
        dv_total = dv_total + shifted(dv_terms[n_back - d], "ctx", -2 * d).astype(F32)
    dv_chip = dv_total.astype(BF16)

    part = half_kv // n_fsdp
    weight_term = None
    for s in range(n_fsdp):
        if s == 0:
            x_tokens = tokens
            dv_part = cols(dv_chip, my_fsdp, part)
        else:
            x_tokens = rotated(tokens, "fsdp", s)
            dv_part = rotated(cols(dv_chip, (my_fsdp + s) % n_fsdp, part), "fsdp", s)
        x_chip = pair(core, x_tokens, swapped(x_tokens), 0)
        term = dot(x_chip, dv_part, TN)
        weight_term = term if weight_term is None else weight_term + term
    groups = [list(range(c, n_ctx, 2)) for c in range(2)]
    rows_chip = lax.psum_scatter(
        weight_term.astype(BF16), "ctx", scatter_dimension=0, axis_index_groups=groups, tiled=True
    )
    rows_out = rows_chip.shape[0] // (2 * n_fsdp)
    blocks = rows_chip.reshape(2, n_fsdp * rows_out, part)
    own = lax.dynamic_index_in_dim(blocks, core, 0, keepdims=False)
    other = swapped(lax.dynamic_index_in_dim(blocks, 1 - core, 0, keepdims=False))
    both = pair(core, own[None], other[None], 0).reshape(2, n_fsdp, rows_out, part)
    gathered = jnp.zeros((n_fsdp, 2, rows_out, part), BF16)
    for s in range(n_fsdp):
        piece = lax.dynamic_index_in_dim(both, (my_fsdp + s) % n_fsdp, 1, keepdims=False)
        if s:
            piece = rotated(piece, "fsdp", s)
        gathered = lax.dynamic_update_index_in_dim(gathered, piece, (my_fsdp - s) % n_fsdp, 0)
    d_weight = jnp.transpose(gathered, (2, 1, 0, 3)).reshape(rows_out, kv_width).astype(F32)

    dv_low = to_tokens(core, dv_chip)
    d_tokens = jnp.zeros((shard_rows, model), BF16)
    for s in range(n_fsdp):
        dv_of = dv_low if s == 0 else rotated(dv_low, "fsdp", s)
        made = dot(dv_of, w_value, NT).astype(BF16)
        if s:
            made = rotated(made, "fsdp", -s)
        d_tokens = lax.dynamic_update_slice_in_dim(d_tokens, made, ((my_fsdp + s) % n_fsdp) * slab, 1)

    out_chip, dq_chip, *dk_terms = run_grads(e, inv, do_t, q_chip, keys, vals)
    dk_total = dk_terms[n_back].astype(F32)
    for d in range(1, n_back + 1):
        dk_total = dk_total + shifted(dk_terms[n_back - d], "ctx", -2 * d).astype(F32)
    return (
        to_tokens(core, out_chip)[None],
        to_tokens(core, dq_chip)[None],
        to_tokens(core, dk_total.astype(BF16))[None],
        d_tokens[None],
        d_weight,
    )


def solution(mesh):
    in_specs = (
        P("fsdp", "ctx", None),
        P("fsdp", "ctx", None),
        P("fsdp", "ctx", None),
        P("fsdp", None),
        P("fsdp", "ctx", None),
        P("fsdp", "ctx"),
    )
    out_specs = (
        P("fsdp", "ctx", None),
        P("fsdp", "ctx", None),
        P("fsdp", "ctx", None),
        P("fsdp", "ctx", None),
        P(("ctx", "fsdp"), None),
    )
    return jax.shard_map(shards, mesh=mesh, in_specs=in_specs, out_specs=out_specs, check_vma=False)
```

time: 450 us -> 303 us (0.67)
  waiting for transfers between devices: 193 us -> 119 us
  matrix products: 83.2 us -> 28.3 us
  starting transfers between devices: 68.7 us -> 38.2 us
  local copies, waits for them, and re-layouts: 63.4 us -> 33.9 us
  Pallas kernels: 0 us -> 28.9 us
  blocking collectives: 0 us -> 18.7 us
    unnamed x3 -> x1, waiting for transfers between devices: 100 us -> 0.02 us
    dot_general x8 -> x6, matrix products: 71 us -> 28.3 us  [dot(): return lax.dot_general(a, b, dims, preferred_element_type=F32)]
    unnamed x42 -> x24, local copies, waits for them, and re-layouts: 37.6 us -> 1.81 us
    ppermute x20 -> x26, starting transfers between devices: 68.7 us -> 38.2 us  [the longest x8 20.7 us: shifted(): lax.ppermute(x, axis, [(i, i + by) for i in range(length) if 0 <= i + by...]
    pallas_call x0 -> x2, Pallas kernels: none -> 28.9 us  [the longest x1 15.4 us: run_grads(): pl.pallas_call(functools.partial(grads_kernel, blk, n_arr - 1), grid=(hea...]
    ppermute x20 -> x26, waiting for transfers between devices: 92.6 us -> 119 us  [the longest x7 60 us: rotated(): lax.ppermute(x, axis, [(i, (i + by) % length) for i in range(length)])]
    all_gather x0 -> x1, blocking collectives: none -> 18.7 us  [shards(): tags = lax.all_gather(segments[0], 'ctx', axis=0, tiled=True)]
    dynamic_update_slice x0 -> x3, local copies, waits for them, and re-layouts: none -> 16.5 us  [the longest x2 14.9 us: shards(): lax.dynamic_update_index_in_dim(gathered, piece, (my_fsdp - s) % n_fsdp, 0)]
  transfers between devices with their start and end apart: 22 -> 27, of which waited for: 11 -> 11; matrix products, arithmetic and copies ran while one was open for 37% -> 22% of each run, Pallas kernels for 0% -> 10%
where the time goes in v1:
time: 303 us; the launch traced here: 300 us
  waiting for transfers between devices  119 us (39%)
  starting transfers between devices  38.2 us (13%)
  local copies, waits for them, and re-layouts  33.9 us (11%)
  Pallas kernels  28.9 us (10%)
  matrix products  28.3 us (9%)
  blocking collectives  18.7 us (6%)
  other arithmetic  17.7 us (6%)
  between operations  14.4 us (5%)
    ppermute x7, waiting for transfers between devices, rotated(): lax.ppermute(x, axis, [(i, (i + by) % length) for i in range(length)])  60 us
    ppermute x8, waiting for transfers between devices, shifted(): lax.ppermute(x, axis, [(i, i + by) for i in range(length) if 0 <= i + by...  58.7 us
    dot_general x6, matrix products, dot(): return lax.dot_general(a, b, dims, preferred_element_type=F32)  28.3 us
    ppermute x8, starting transfers between devices, shifted(): lax.ppermute(x, axis, [(i, i + by) for i in range(length) if 0 <= i + by...  20.7 us
    all_gather x1, blocking collectives, shards(): tags = lax.all_gather(segments[0], 'ctx', axis=0, tiled=True)  18.7 us
    pallas_call x1, Pallas kernels, run_grads(): pl.pallas_call(functools.partial(grads_kernel, blk, n_arr - 1), grid=(hea...  15.4 us
    dynamic_update_slice x2, local copies, waits for them, and re-layouts, shards(): lax.dynamic_update_index_in_dim(gathered, piece, (my_fsdp - s) % n_fsdp, 0)  14.9 us
    pallas_call x1, Pallas kernels, run_probs(): pl.pallas_call(functools.partial(probs_kernel, blk, n_arr - 1), grid=(hea...  13.5 us
  transfers between devices with their start and end apart: 27, of which 11 were waited for; matrix products, arithmetic and copies ran while one was open for 22% of the time, Pallas kernels for 10%

profile of v1, /device:TPU:9, one launch (start us, length us, event | category | flops | bytes accessed | tf_op | source)
XLA Modules:
  0.0 299.6 jit_solution(11056621419080940654)
XLA Ops:
  7.2 1.3 collective-permute-start.21
  10.6 2.2 dynamic-slice_bitcast_fusion.6
  14.2 18.7 %all-gather = s32[1,4096]{1,0:T(1,128)S(1)} all-gather(s32[1,256]{1,0:T(1,128)S(1)} %copy-done.9), channel_id=2, replica_groups=mesh['ctx'=16,'fsdp'=2] {'ctx'}, dimensions={1}, use_global_device_ids=true | all-gather | bytes 17408 | tf_op jit(solution)/shard_map/all_gather | solution.py:271
  33.1 1.9 collective-permute-start.3
  35.0 1.9 collective-permute-start.4
  38.3 2.1 maximum_select_fusion.4.q_ref
  40.4 1.7 maximum_select_fusion.5.do_ref
  42.0 26.1 %collective-permute-done.21 = bf16[256,5376]{1,0:T(8,128)(2,1)} collective-permute-done((bf16[256,5376]{1,0:T(8,128)(2,1)}, bf16[256,5376]{1,0:T(8,128)(2,1)}, u32[]{:S(2)}, u32[]{:S(2)}) %collective-permute-start.21) | collective-permute-done | bytes 2752544 | tf_op jit(solution)/shard_map/ppermute | solution.py:217
  68.2 1.5 collective-permute-start.22
  69.7 13.5 %probs.1 = (bf16[4,2,1280,512]{3,2,1,0:T(8,128)(2,1)}, f32[4,2,1,512]{3,2,1,0:T(1,128)S(1)}, bf16[4,2,128,512]{3,2,1,0:T(8,128)(2,1)S(1)}, bf16[512,512]{1,0:T(8...) custom-call(s32[1,512]{1,0:T(1,128)S(1)} %maximum_subtract_fusion.low_ref, ...), custom_call_target="tpu_custom_call" | custom-call | flops 16106127360 | bytes 10485760 | tf_op jit(solution)/shard_map/probs/pallas_call | solution.py:142
  84.2 1.9 collective-permute-start.16
  86.1 2.6 collective-permute-start.15
  88.7 11.2 %collective-permute-done.16 = bf16[512,512]{1,0:T(8,128)(2,1)} collective-permute-done((bf16[512,512]{1,0:T(8,128)(2,1)}, bf16[512,512]{1,0:T(8,128)(2,1)}, u32[]{:S(2)}, u32[]{:S(2)}) %collective-permute-start.16) | collective-permute-done | bytes 524320 | tf_op jit(solution)/shard_map/ppermute | solution.py:208
  99.9 9.1 %collective-permute-done.15 = bf16[512,512]{1,0:T(8,128)(2,1)} collective-permute-done((bf16[512,512]{1,0:T(8,128)(2,1)}, bf16[512,512]{1,0:T(8,128)(2,1)}, u32[]{:S(2)}, u32[]{:S(2)}) %collective-permute-start.15) | collective-permute-done | bytes 524320 | tf_op jit(solution)/shard_map/ppermute | solution.py:208
  109.1 1.4 add_convert_fusion
  111.3 1.3 collective-permute-start.23
  112.6 2.5 dynamic-slice_bitcast_fusion
  115.3 3.3 %collective-permute-done.23 = bf16[512,256]{1,0:T(8,128)(2,1)} collective-permute-done((bf16[512,256]{1,0:T(8,128)(2,1)S(1)}, bf16[512,256]{1,0:T(8,128)(2,1)}, u32[]{:S(2)}, u32[]{:S(2)}) %collective-permute-start.23) | collective-permute-done | bytes 262176 | tf_op jit(solution)/shard_map/ppermute | solution.py:217
  118.6 5.5 %fusion.6 = f32[5376,256]{1,0:T(8,128)S(1)} fusion(bf16[512,256]{1,0:T(8,128)(2,1)} %collective-permute-done.23, bf16[256,5376]{1,0:T(8,128)(2,1)} %collective-permute-done.22, bf16[256,5376]{1,0:T(8,128)(2,1)} %collective-permute-done.21, pred[]{:T(512)S(6)} %eq.12), kind=kOutput, calls=%fused_computation.10 | convolution fusion | flops 1434058752 | bytes 11272193 | tf_op jit(solution)/shard_map/dot_general | solution.py:28
  124.1 5.3 %fusion = bf16[5376,256]{1,0:T(8,128)(2,1)} fusion(f32[5376,256]{1,0:T(8,128)S(1)} %fusion.6, bf16[256,5376]{1,0:T(8,128)(2,1)} %collective-permute-done.20, bf16[256,5376]{1,0:T(8,128)(2,1)S(1)} %bitcast.58, pred[]{:T(512)S(6)} %eq.12, bf16[512,512]{1,0:T(8,128)(2,1)S(1)} %copy-done.3, s32[]{:T(128)S(6)} %select_n.221), kind=kOutput, calls=%fused_computation.2 | convolution fusion | flops 1436811264 | bytes 14024709 | tf_op jit(solution)/shard_map/dot_general | solution.py:28
  129.4 18.6 %collective-permute-done.5 = bf16[256,2688]{1,0:T(8,128)(2,1)} collective-permute-done((bf16[256,2688]{1,0:T(8,128)(2,1)}, bf16[256,2688]{1,0:T(8,128)(2,1)}, u32[]{:S(2)}, u32[]{:S(2)}) %collective-permute-start.5) | collective-permute-done | bytes 1376288 | tf_op jit(solution)/shard_map/ppermute | solution.py:217
  148.1 5.5 %convolution_convert_fusion.2 = bf16[256,1024]{1,0:T(8,128)(2,1)} fusion(bf16[256,2688]{1,0:T(8,128)(2,1)} %collective-permute-done.5, bf16[2688,1024]{1,0:T(8,128)(2,1)} %param.9), kind=kOutput, calls=%fused_computation.27 | convolution fusion | flops 1409548288 | bytes 7405568 | tf_op jit(solution)/shard_map/dot_general | solution.py:28
  154.8 4.7 %fusion.16 = f32[256,1024]{1,0:T(8,128)S(1)} fusion(bf16[2688,1024]{1,0:T(8,128)(2,1)} %param.9, bf16[1,256,5376]{2,1,0:T(8,128)(2,1)} %param.6, s32[]{:T(128)S(6)} %select_n.204), kind=kOutput, calls=%fused_computation.23 | convolution fusion | flops 1409286144 | bytes 7929860 | tf_op jit(solution)/shard_map/dot_general | solution.py:28
  159.5 6.2 %collective-permute-done.6 = bf16[256,1024]{1,0:T(8,128)(2,1)} collective-permute-done((bf16[256,1024]{1,0:T(8,128)(2,1)}, bf16[256,1024]{1,0:T(8,128)(2,1)}, u32[]{:S(2)}, u32[]{:S(2)}) %collective-permute-start.6) | collective-permute-done | bytes 524320 | tf_op jit(solution)/shard_map/ppermute | solution.py:217
  167.7 2.5 collective-permute-start.7
  172.9 3.2 %collective-permute-start.8 = (bf16[512,512]{1,0:T(8,128)(2,1)S(1)}, bf16[512,512]{1,0:T(8,128)(2,1)S(1)}, u32[]{:S(2)}, u32[]{:S(2)}) collective-permute-start(bf16[512,512]{1,0:T(8,128)(2,1)S(1)} %maximum_select_fusion.9.refs_5_), channel_id=1, source_target_pairs={{0,8},{2,10},{4,12},{6,14},{8,16},{10,18},{12,20},{14,22},{16,24},... | collective-permute-start | bytes 1572872 | tf_op jit(solution)/shard_map/ppermute | solution.py:208
  176.1 5.2 %collective-permute-start.9 = (bf16[512,512]{1,0:T(8,128)(2,1)S(1)}, bf16[512,512]{1,0:T(8,128)(2,1)S(1)}, u32[]{:S(2)}, u32[]{:S(2)}) collective-permute-start(bf16[512,512]{1,0:T(8,128)(2,1)S(1)} %maximum_select_fusion.9.refs_5_), channel_id=1, source_target_pairs={{0,4},{2,6},{4,8},{6,10},{8,12},{10,14},{12,16},{14,18},{16,20},{1... | collective-permute-start | bytes 1572872 | tf_op jit(solution)/shard_map/ppermute | solution.py:208
  182.5 1.3 collective-permute-start.18
  183.9 4.4 %fusion.15 = bf16[1,256,5376]{2,1,0:T(8,128)(2,1)S(1)} fusion(bf16[1,256,5376]{2,1,0:T(8,128)(2,1)S(1)} %broadcast_in_dim.26, s32[]{:T(128)S(6)} %select_n.217, bf16[256,1024]{1,0:T(8,128)(2,1)S(1)} %maximum_select_fusion.11, bf16[2688,1024]{1,0:T(8,128)(2,1)} %param.9), kind=kOutput, calls=%fused_computation.21 | convolution fusion | flops 1409974272 | bytes 7405572 | tf_op jit(solution)/shard_map/dot_general | solution.py:28
  188.4 23.0 %collective-permute-done.9.refs_4_ = bf16[512,512]{1,0:T(8,128)(2,1)S(1)} collective-permute-done((bf16[512,512]{1,0:T(8,128)(2,1)S(1)}, bf16[512,512]{1,0:T(8,128)(2,1)S(1)}, u32[]{:S(2)}, u32[]{:S(2)}) %collective-permute-start.9) | collective-permute-done | bytes 524320 | tf_op jit(solution)/shard_map/ppermute | solution.py:208
  211.5 15.4 %grads.1 = (bf16[512,1024]{1,0:T(8,128)(2,1)S(1)}, bf16[512,1024]{1,0:T(8,128)(2,1)S(1)}, bf16[512,512]{1,0:T(8,128)(2,1)S(1)}, bf16[512,512]{1,0:T(8,128)(2,1)S(1)}, bf16[512,512]{1,0:T(8,128)(2,1)S(1)}) custom-call(bf16[4,2,1280,512]{3,2,1,0:T(8,128)(2,1)} %get-tuple-element.16.e_ref, f32[4,2,1,512]{3,2,1,0:T(1,128)S(1)} %get-tuple-element.17.inv_ref, ...), custom_call_target="tpu_custom_call" | custom-call | flops 21474836480 | bytes 10485760 | tf_op jit(solution)/shard_map/grads/pallas_call | solution.py:182
  227.0 2.9 collective-permute-start.10
  229.9 1.9 collective-permute-start.13
  231.8 2.1 collective-permute-start.12
  234.0 2.8 convolution_convert_fusion
  236.8 1.3 collective-permute-start.19
  239.2 6.1 %collective-permute-done.13 = bf16[512,512]{1,0:T(8,128)(2,1)S(1)} collective-permute-done((bf16[512,512]{1,0:T(8,128)(2,1)S(1)}, bf16[512,512]{1,0:T(8,128)(2,1)S(1)}, u32[]{:S(2)}, u32[]{:S(2)}) %collective-permute-start.13) | collective-permute-done | bytes 524320 | tf_op jit(solution)/shard_map/ppermute | solution.py:208
  245.4 9.1 %collective-permute-done.12 = bf16[512,512]{1,0:T(8,128)(2,1)S(1)} collective-permute-done((bf16[512,512]{1,0:T(8,128)(2,1)S(1)}, bf16[512,512]{1,0:T(8,128)(2,1)S(1)}, u32[]{:S(2)}, u32[]{:S(2)}) %collective-permute-start.12) | collective-permute-done | bytes 524320 | tf_op jit(solution)/shard_map/ppermute | solution.py:208
  256.1 1.4 maximum_select_fusion.6
  258.6 2.6 maximum_select_fusion.7
  261.9 1.3 collective-permute-start.25
  263.2 5.7 %collective-permute-done.19 = bf16[256,2688]{1,0:T(8,128)(2,1)} collective-permute-done((bf16[256,2688]{1,0:T(8,128)(2,1)}, bf16[256,2688]{1,0:T(8,128)(2,1)}, u32[]{:S(2)}, u32[]{:S(2)}) %collective-permute-start.19) | collective-permute-done | bytes 1376288 | tf_op jit(solution)/shard_map/ppermute | solution.py:217
  268.9 1.5 bitcast_dynamic-update-slice_fusion
  270.4 2.4 maximum_select_fusion.10
  274.0 7.5 %dynamic_update_slice.17 = bf16[2,2,168,256]{3,0,1,2:T(2,128)(2,1)} dynamic-update-slice(bf16[2,2,168,256]{3,0,1,2:T(2,128)(2,1)} %broadcast_in_dim.29, bf16[1,2,168,256]{3,0,1,2:T(2,128)(2,1)S(1)} %copy.13, s32[]{:T(128)S(6)} %select_n.227, s32[]{:T(128)} %constant.94.clone.1, s32[]{:T(128)} %constant.94.clone.1, s32[]{:T(128)} %constant.94.clone.1) | dynamic-update-slice | bytes 344068 | tf_op jit(solution)/shard_map/jit(dynamic_update_index_in_dim)/dynamic_update_slice | solution.py:310
  282.7 7.5 %dynamic_update_slice.18 = bf16[2,2,168,256]{3,0,1,2:T(2,128)(2,1)} dynamic-update-slice(bf16[2,2,168,256]{3,0,1,2:T(2,128)(2,1)} %dynamic_update_slice.17, bf16[1,2,168,256]{3,0,1,2:T(2,128)(2,1)S(1)} %copy.14, s32[]{:T(128)S(6)} %select_n.230, s32[]{:T(128)} %constant.94.clone.1, s32[]{:T(128)} %constant.94.clone.1, s32[]{:T(128)} %constant.94.clone.1) | dynamic-update-slice | bytes 344068 | tf_op jit(solution)/shard_map/jit(dynamic_update_index_in_dim)/dynamic_update_slice | solution.py:310
  290.1 1.2 convert_bitcast_fusion
  291.4 1.4 reshape.224
  (77 shorter events, 21.2 us)
Async XLA Ops:
  7.2 5.7 %copy-start.7 = (bf16[1,256,2048]{2,1,0:T(8,128)(2,1)S(1)}, bf16[1,256,2048]{2,1,0:T(8,128)(2,1)}, u32[]{:S(2)}) copy-start(bf16[1,256,2048]{2,1,0:T(8,128)(2,1)} %param.10) | copy-start | bytes 3145732
  7.2 7.0 %copy-start.9 = (s32[1,256]{1,0:T(1,128)S(1)}, s32[1,256]{1,0:T(1,128)}, u32[]{:S(2)}) copy-start(s32[1,256]{1,0:T(1,128)} %param.11) | copy-start | bytes 3076
  7.2 250.3 %reduce-scatter.2.cloned.1.call-start = ((), (), s32[]{:S(2)}) async-start(), calls=%async_computation.1 | async-start | bytes 3096576 | tf_op jit(solution)/shard_map/reduce_scatter | solution.py:297
  7.2 60.9 %collective-permute-start.21 = (bf16[256,5376]{1,0:T(8,128)(2,1)}, bf16[256,5376]{1,0:T(8,128)(2,1)}, u32[]{:S(2)}, u32[]{:S(2)}) collective-permute-start(bf16[256,5376]{1,0:T(8,128)(2,1)} %bitcast.56), channel_id=1, source_target_pairs={{0,1},{1,0},{2,3},{3,2},{4,5},{5,4},{6,7},{7,6},{8,9},{9,8},{10,11... | collective-permute-start | bytes 8257544 | tf_op jit(solution)/shard_map/ppermute | solution.py:217
  9.6 23.3 %collective-permute-start.2 = (bf16[256,512]{1,0:T(8,128)(2,1)S(1)}, bf16[256,512]{1,0:T(8,128)(2,1)S(1)}, u32[]{:S(2)}, u32[]{:S(2)}) collective-permute-start(bf16[256,512]{1,0:T(8,128)(2,1)S(1)} %get-tuple-element.42), channel_id=1, source_target_pairs={{0,2},{2,0},{4,6},{6,4},{8,10},{10,8},{12,14},{14,12},{16,18},{18,... | collective-permute-start | bytes 786440 | tf_op jit(solution)/shard_map/ppermute | solution.py:212
  12.8 25.2 %collective-permute-start = (bf16[256,1024]{1,0:T(8,128)(2,1)}, bf16[256,1024]{1,0:T(8,128)(2,1)}, u32[]{:S(2)}, u32[]{:S(2)}) collective-permute-start(bf16[256,1024]{1,0:T(8,128)(2,1)} %get-tuple-element.34), channel_id=1, source_target_pairs={{0,2},{2,0},{4,6},{6,4},{8,10},{10,8},{12,14},{14,12},{16,18},{18,... | collective-permute-start | bytes 1572872 | tf_op jit(solution)/shard_map/ppermute | solution.py:212
  13.7 26.6 %collective-permute-start.1 = (bf16[256,1024]{1,0:T(8,128)(2,1)}, bf16[256,1024]{1,0:T(8,128)(2,1)}, u32[]{:S(2)}, u32[]{:S(2)}) collective-permute-start(bf16[256,1024]{1,0:T(8,128)(2,1)} %get-tuple-element.32), channel_id=1, source_target_pairs={{0,2},{2,0},{4,6},{6,4},{8,10},{10,8},{12,14},{14,12},{16,18},{18,... | collective-permute-start | bytes 1572872 | tf_op jit(solution)/shard_map/ppermute | solution.py:212
  33.1 36.6 %collective-permute-start.3 = (bf16[512,512]{1,0:T(8,128)(2,1)S(1)}, bf16[512,512]{1,0:T(8,128)(2,1)S(1)}, u32[]{:S(2)}, u32[]{:S(2)}) collective-permute-start(bf16[512,512]{1,0:T(8,128)(2,1)S(1)} %maximum_select_fusion.8.refs_2_), channel_id=1, source_target_pairs={{0,8},{2,10},{4,12},{6,14},{8,16},{10,18},{12,20},{14,22},{16,24},... | collective-permute-start | bytes 1572872 | tf_op jit(solution)/shard_map/ppermute | solution.py:208
  35.0 34.7 %collective-permute-start.4 = (bf16[512,512]{1,0:T(8,128)(2,1)S(1)}, bf16[512,512]{1,0:T(8,128)(2,1)S(1)}, u32[]{:S(2)}, u32[]{:S(2)}) collective-permute-start(bf16[512,512]{1,0:T(8,128)(2,1)S(1)} %maximum_select_fusion.8.refs_2_), channel_id=1, source_target_pairs={{0,4},{2,6},{4,8},{6,10},{8,12},{10,14},{12,16},{14,18},{16,20},{1... | collective-permute-start | bytes 1572872 | tf_op jit(solution)/shard_map/ppermute | solution.py:208
  38.0 86.1 %collective-permute-start.20 = (bf16[256,5376]{1,0:T(8,128)(2,1)}, bf16[256,5376]{1,0:T(8,128)(2,1)}, u32[]{:S(2)}, u32[]{:S(2)}) collective-permute-start(bf16[256,5376]{1,0:T(8,128)(2,1)} %bitcast.57), channel_id=1, source_target_pairs={{0,2},{2,0},{4,6},{6,4},{8,10},{10,8},{12,14},{14,12},{16,18},{18,... | collective-permute-start | bytes 8257544 | tf_op jit(solution)/shard_map/ppermute | solution.py:212
  68.2 50.5 %collective-permute-start.22 = (bf16[256,5376]{1,0:T(8,128)(2,1)}, bf16[256,5376]{1,0:T(8,128)(2,1)}, u32[]{:S(2)}, u32[]{:S(2)}) collective-permute-start(bf16[256,5376]{1,0:T(8,128)(2,1)} %collective-permute-done.21), channel_id=1, source_target_pairs={{0,2},{2,0},{4,6},{6,4},{8,10},{10,8},{12,14},{14,12},{16,18},{18,... | collective-permute-start | bytes 8257544 | tf_op jit(solution)/shard_map/ppermute | solution.py:212
  83.2 1.0 copy-start
  84.2 15.7 %collective-permute-start.16 = (bf16[512,512]{1,0:T(8,128)(2,1)}, bf16[512,512]{1,0:T(8,128)(2,1)}, u32[]{:S(2)}, u32[]{:S(2)}) collective-permute-start(bf16[512,512]{1,0:T(8,128)(2,1)} %get-tuple-element.26), channel_id=1, source_target_pairs={{8,0},{10,2},{12,4},{14,6},{16,8},{18,10},{20,12},{22,14},{24,16},... | collective-permute-start | bytes 1572872 | tf_op jit(solution)/shard_map/ppermute | solution.py:208
  86.1 23.0 %collective-permute-start.15 = (bf16[512,512]{1,0:T(8,128)(2,1)}, bf16[512,512]{1,0:T(8,128)(2,1)}, u32[]{:S(2)}, u32[]{:S(2)}) collective-permute-start(bf16[512,512]{1,0:T(8,128)(2,1)} %get-tuple-element.25), channel_id=1, source_target_pairs={{4,0},{6,2},{8,4},{10,6},{12,8},{14,10},{16,12},{18,14},{20,16},{2... | collective-permute-start | bytes 1572872 | tf_op jit(solution)/shard_map/ppermute | solution.py:208
  110.5 0.8 copy-start.2
  111.3 7.3 %collective-permute-start.23 = (bf16[512,256]{1,0:T(8,128)(2,1)S(1)}, bf16[512,256]{1,0:T(8,128)(2,1)}, u32[]{:S(2)}, u32[]{:S(2)}) collective-permute-start(bf16[512,256]{1,0:T(8,128)(2,1)S(1)} %constant_dynamic-slice_fusion.2), channel_id=1, source_target_pairs={{0,1},{1,0},{2,3},{3,2},{4,5},{5,4},{6,7},{7,6},{8,9},{9,8},{10,11... | collective-permute-start | bytes 786440 | tf_op jit(solution)/shard_map/ppermute | solution.py:217
  115.1 33.0 %collective-permute-start.5 = (bf16[256,2688]{1,0:T(8,128)(2,1)}, bf16[256,2688]{1,0:T(8,128)(2,1)}, u32[]{:S(2)}, u32[]{:S(2)}) collective-permute-start(bf16[256,2688]{1,0:T(8,128)(2,1)} %dynamic-slice_bitcast_fusion), channel_id=1, source_target_pairs={{0,1},{1,0},{2,3},{3,2},{4,5},{5,4},{6,7},{7,6},{8,9},{9,8},{10,11... | collective-permute-start | bytes 4128776 | tf_op jit(solution)/shard_map/ppermute | solution.py:217
  115.3 8.8 %copy-start.3 = (bf16[512,512]{1,0:T(8,128)(2,1)S(1)}, bf16[512,512]{1,0:T(8,128)(2,1)}, u32[]{:S(2)}) copy-start(bf16[512,512]{1,0:T(8,128)(2,1)} %copy-done.2) | copy-start | bytes 1572868
  115.3 8.8 %copy-start.8 = (bf16[1,256,5376]{2,1,0:T(8,128)(2,1)S(1)}, bf16[1,256,5376]{2,1,0:T(8,128)(2,1)}, u32[]{:S(2)}) copy-start(bf16[1,256,5376]{2,1,0:T(8,128)(2,1)} %param.6) | copy-start | bytes 8257540
  153.6 12.2 %collective-permute-start.6 = (bf16[256,1024]{1,0:T(8,128)(2,1)}, bf16[256,1024]{1,0:T(8,128)(2,1)}, u32[]{:S(2)}, u32[]{:S(2)}) collective-permute-start(bf16[256,1024]{1,0:T(8,128)(2,1)} %convolution_convert_fusion.2), channel_id=1, source_target_pairs={{0,1},{1,0},{2,3},{3,2},{4,5},{5,4},{6,7},{7,6},{8,9},{9,8},{10,11... | collective-permute-start | bytes 1572872 | tf_op jit(solution)/shard_map/ppermute | solution.py:217
  167.7 4.0 %collective-permute-start.7 = (bf16[256,512]{1,0:T(8,128)(2,1)}, bf16[256,512]{1,0:T(8,128)(2,1)}, u32[]{:S(2)}, u32[]{:S(2)}) collective-permute-start(bf16[256,512]{1,0:T(8,128)(2,1)} %get-tuple-element.40), channel_id=1, source_target_pairs={{0,2},{2,0},{4,6},{6,4},{8,10},{10,8},{12,14},{14,12},{16,18},{18,... | collective-permute-start | bytes 786440 | tf_op jit(solution)/shard_map/ppermute | solution.py:212
  171.1 10.2 %collective-permute-start.17 = (bf16[256,512]{1,0:T(8,128)(2,1)}, bf16[256,512]{1,0:T(8,128)(2,1)S(1)}, u32[]{:S(2)}, u32[]{:S(2)}) collective-permute-start(bf16[256,512]{1,0:T(8,128)(2,1)} %get-tuple-element.36), channel_id=1, source_target_pairs={{0,2},{2,0},{4,6},{6,4},{8,10},{10,8},{12,14},{14,12},{16,18},{18,... | collective-permute-start | bytes 786440 | tf_op jit(solution)/shard_map/ppermute | solution.py:212
  172.9 15.5 %collective-permute-start.8 = (bf16[512,512]{1,0:T(8,128)(2,1)S(1)}, bf16[512,512]{1,0:T(8,128)(2,1)S(1)}, u32[]{:S(2)}, u32[]{:S(2)}) collective-permute-start(bf16[512,512]{1,0:T(8,128)(2,1)S(1)} %maximum_select_fusion.9.refs_5_), channel_id=1, source_target_pairs={{0,8},{2,10},{4,12},{6,14},{8,16},{10,18},{12,20},{14,22},{16,24},... | collective-permute-start | bytes 1572872 | tf_op jit(solution)/shard_map/ppermute | solution.py:208
  176.1 35.3 %collective-permute-start.9 = (bf16[512,512]{1,0:T(8,128)(2,1)S(1)}, bf16[512,512]{1,0:T(8,128)(2,1)S(1)}, u32[]{:S(2)}, u32[]{:S(2)}) collective-permute-start(bf16[512,512]{1,0:T(8,128)(2,1)S(1)} %maximum_select_fusion.9.refs_5_), channel_id=1, source_target_pairs={{0,4},{2,6},{4,8},{6,10},{8,12},{10,14},{12,16},{14,18},{16,20},{1... | collective-permute-start | bytes 1572872 | tf_op jit(solution)/shard_map/ppermute | solution.py:208
  182.5 51.5 %collective-permute-start.18 = (bf16[256,1024]{1,0:T(8,128)(2,1)S(1)}, bf16[256,1024]{1,0:T(8,128)(2,1)S(1)}, u32[]{:S(2)}, u32[]{:S(2)}) collective-permute-start(bf16[256,1024]{1,0:T(8,128)(2,1)S(1)} %maximum_select_fusion.11), channel_id=1, source_target_pairs={{0,1},{1,0},{2,3},{3,2},{4,5},{5,4},{6,7},{7,6},{8,9},{9,8},{10,11... | collective-permute-start | bytes 1572872 | tf_op jit(solution)/shard_map/ppermute | solution.py:217
  183.9 27.5 %copy-start.1 = (bf16[4,2,128,512]{3,2,1,0:T(8,128)(2,1)S(1)}, bf16[4,2,128,512]{3,2,1,0:T(8,128)(2,1)}, u32[]{:S(2)}) copy-start(bf16[4,2,128,512]{3,2,1,0:T(8,128)(2,1)} %copy-done) | copy-start | bytes 3145732
  183.9 50.0 %slice-start = ((s8[5505024]{0:T(1024)(128)(4,1)}), s8[4194304]{0:T(1024)(128)(4,1)S(1)}, s32[]{:S(2)}) async-start(s8[5505024]{0:T(1024)(128)(4,1)} %bitcast.66), calls=%async_computation.2 | async-start | bytes 8388608
  188.4 23.1 %copy-start.4 = (bf16[1,256,5376]{2,1,0:T(8,128)(2,1)}, bf16[1,256,5376]{2,1,0:T(8,128)(2,1)S(1)}, u32[]{:S(2)}) copy-start(bf16[1,256,5376]{2,1,0:T(8,128)(2,1)S(1)} %fusion.15) | copy-start | bytes 8257540
  211.5 22.5 %slice-start.1 = ((s8[5505024]{0:T(1024)(128)(4,1)}), s8[1310720]{0:T(1024)(128)(4,1)S(1)}, s32[]{:S(2)}) async-start(s8[5505024]{0:T(1024)(128)(4,1)} %bitcast.66), calls=%async_computation.3 | async-start | bytes 2621440
  227.0 29.1 %collective-permute-start.10 = (bf16[256,1024]{1,0:T(8,128)(2,1)S(1)}, bf16[256,1024]{1,0:T(8,128)(2,1)S(1)}, u32[]{:S(2)}, u32[]{:S(2)}) collective-permute-start(bf16[256,1024]{1,0:T(8,128)(2,1)S(1)} %get-tuple-element.30), channel_id=1, source_target_pairs={{0,2},{2,0},{4,6},{6,4},{8,10},{10,8},{12,14},{14,12},{16,18},{18,... | collective-permute-start | bytes 1572872 | tf_op jit(solution)/shard_map/ppermute | solution.py:212
  229.9 15.5 %collective-permute-start.13 = (bf16[512,512]{1,0:T(8,128)(2,1)S(1)}, bf16[512,512]{1,0:T(8,128)(2,1)S(1)}, u32[]{:S(2)}, u32[]{:S(2)}) collective-permute-start(bf16[512,512]{1,0:T(8,128)(2,1)S(1)} %get-tuple-element.23), channel_id=1, source_target_pairs={{8,0},{10,2},{12,4},{14,6},{16,8},{18,10},{20,12},{22,14},{24,16},... | collective-permute-start | bytes 1572872 | tf_op jit(solution)/shard_map/ppermute | solution.py:208
  231.8 22.7 %collective-permute-start.12 = (bf16[512,512]{1,0:T(8,128)(2,1)S(1)}, bf16[512,512]{1,0:T(8,128)(2,1)S(1)}, u32[]{:S(2)}, u32[]{:S(2)}) collective-permute-start(bf16[512,512]{1,0:T(8,128)(2,1)S(1)} %get-tuple-element.22), channel_id=1, source_target_pairs={{4,0},{6,2},{8,4},{10,6},{12,8},{14,10},{16,12},{18,14},{20,16},{2... | collective-permute-start | bytes 1572872 | tf_op jit(solution)/shard_map/ppermute | solution.py:208
  236.8 32.1 %collective-permute-start.19 = (bf16[256,2688]{1,0:T(8,128)(2,1)}, bf16[256,2688]{1,0:T(8,128)(2,1)}, u32[]{:S(2)}, u32[]{:S(2)}) collective-permute-start(bf16[256,2688]{1,0:T(8,128)(2,1)} %convolution_convert_fusion), channel_id=1, source_target_pairs={{0,1},{1,0},{2,3},{3,2},{4,5},{5,4},{6,7},{7,6},{8,9},{9,8},{10,11... | collective-permute-start | bytes 4128776 | tf_op jit(solution)/shard_map/ppermute | solution.py:217
  238.9 19.6 %collective-permute-start.11 = (bf16[256,1024]{1,0:T(8,128)(2,1)}, bf16[256,1024]{1,0:T(8,128)(2,1)}, u32[]{:S(2)}, u32[]{:S(2)}) collective-permute-start(bf16[256,1024]{1,0:T(8,128)(2,1)} %get-tuple-element.28), channel_id=1, source_target_pairs={{0,2},{2,0},{4,6},{6,4},{8,10},{10,8},{12,14},{14,12},{16,18},{18,... | collective-permute-start | bytes 1572872 | tf_op jit(solution)/shard_map/ppermute | solution.py:212
  255.5 15.0 %collective-permute-start.14 = (bf16[256,512]{1,0:T(8,128)(2,1)}, bf16[256,512]{1,0:T(8,128)(2,1)}, u32[]{:S(2)}, u32[]{:S(2)}) collective-permute-start(bf16[256,512]{1,0:T(8,128)(2,1)} %get-tuple-element.38), channel_id=1, source_target_pairs={{0,2},{2,0},{4,6},{6,4},{8,10},{10,8},{12,14},{14,12},{16,18},{18,... | collective-permute-start | bytes 786440 | tf_op jit(solution)/shard_map/ppermute | solution.py:212
  256.1 12.8 %copy-start.5 = (bf16[1,256,5376]{2,1,0:T(8,128)(2,1)S(1)}, bf16[1,256,5376]{2,1,0:T(8,128)(2,1)}, u32[]{:S(2)}) copy-start(bf16[1,256,5376]{2,1,0:T(8,128)(2,1)} %copy-done.4) | copy-start | bytes 8257540
  258.5 2.7 collective-permute-start.24
  261.9 19.6 %collective-permute-start.25 = (bf16[2,168,256]{2,1,0:T(8,128)(2,1)}, bf16[2,168,256]{2,1,0:T(8,128)(2,1)}, u32[]{:S(2)}, u32[]{:S(2)}) collective-permute-start(bf16[2,168,256]{2,1,0:T(8,128)(2,1)} %get-tuple-element.43), channel_id=1, source_target_pairs={{0,1},{1,0},{2,3},{3,2},{4,5},{5,4},{6,7},{7,6},{8,9},{9,8},{10,11... | collective-permute-start | bytes 516104 | tf_op jit(solution)/shard_map/ppermute | solution.py:217
  270.4 22.3 %copy-start.6 = (bf16[1,256,5376]{2,1,0:T(8,128)(2,1)}, bf16[1,256,5376]{2,1,0:T(8,128)(2,1)S(1)}, u32[]{:S(2)}) copy-start(bf16[1,256,5376]{2,1,0:T(8,128)(2,1)S(1)} %bitcast_dynamic-update-slice_fusion) | copy-start | bytes 8257540
Sparse Core Ops, SparseCore 0:
  129.6 77.0 reduce-scatter.1

commit v2 on v1

v2 whole, which is shorter than its diff:
```python
import functools
import math

import jax
import jax.numpy as jnp
from jax import lax
from jax.experimental import pallas as pl
from jax.experimental.pallas import tpu as pltpu
from jax.sharding import PartitionSpec as P

HQ = 16
HK = 8
HD = 128
WINDOW = 1024
GROUP = 2
NEG = -1e30

score_scale = 1.0 / math.sqrt(168.0)
exp2_scale = score_scale / math.log(2.0)

BF16 = jnp.bfloat16
F32 = jnp.float32
NT = (((1,), (1,)), ((), ()))
TN = (((0,), (0,)), ((), ()))


def dot(a, b, dims=(((1,), (0,)), ((), ()))):
    return lax.dot_general(a, b, dims, preferred_element_type=F32)


def probs_kernel(blk, n_back, core_ref, low_ref, q_own, q_other, do_own, do_other, *refs):
    n_arr = n_back + 1
    k_refs = refs[:n_arr]
    e_ref, inv_ref, dot_ref = refs[n_arr : n_arr + 3]
    dv_refs = refs[n_arr + 3 : 2 * n_arr + 3]
    bias, s_scr, dv_acc, q_buf, do_buf = refs[2 * n_arr + 3 :]
    span_blocks = WINDOW // blk + 1
    core = core_ref[0]

    @pl.when(pl.program_id(0) == 0)
    def _():
        for qb in range(2):
            kpos = lax.broadcasted_iota(jnp.int32, (span_blocks * blk, blk), 0) + qb * blk
            qpos = lax.broadcasted_iota(jnp.int32, (span_blocks * blk, blk), 1) + (qb * blk + WINDOW)
            low = low_ref[:, qb * blk : (qb + 1) * blk]
            ok = (kpos >= low) & (kpos <= qpos)
            bias[qb] = jnp.where(ok, 0.0, NEG)

    q_buf[core] = q_own[...]
    q_buf[1 - core] = q_other[...]
    do_buf[core] = do_own[...]
    do_buf[1 - core] = do_other[...]

    def key_block(j):
        return k_refs[j // 2][(j % 2) * blk : (j % 2 + 1) * blk, :]

    def stacked(buf, qb):
        return jnp.concatenate([buf[qb, :, r * HD : (r + 1) * HD] for r in range(GROUP)], 0)

    for qb in range(2):
        qs = stacked(q_buf, qb)
        top = None
        for j in range(span_blocks):
            s = dot(key_block(qb + j), qs, NT)
            b = bias[qb, j * blk : (j + 1) * blk, :]
            s = s * exp2_scale + jnp.concatenate([b] * GROUP, 1)
            s_scr[j] = s
            part = jnp.max(s.reshape(blk // 8, 8, GROUP * blk), axis=0)
            top = part if top is None else jnp.maximum(top, part)
        top = jnp.max(top, axis=0, keepdims=True)
        total = None
        for j in range(span_blocks):
            e = jnp.exp2(s_scr[j] - top)
            part = jnp.sum(e.reshape(blk // 8, 8, GROUP * blk), axis=0)
            total = part if total is None else total + part
            e_ref[0, qb, j * blk : (j + 1) * blk, :] = e.astype(BF16)
        inv = 1.0 / jnp.sum(total, axis=0, keepdims=True)
        inv_ref[0, qb] = inv
        do_t = (stacked(do_buf, qb).astype(F32).T * inv).astype(BF16)
        dot_ref[0, qb] = do_t
        for j in range(span_blocks):
            term = dot(e_ref[0, qb, j * blk : (j + 1) * blk, :], do_t, NT)
            at = slice((qb + j) * blk, (qb + j + 1) * blk)
            if qb == 0 or j == span_blocks - 1:
                dv_acc[at, :] = term
            else:
                dv_acc[at, :] += term
    for a in range(n_arr):
        dv_refs[a][...] = dv_acc[a * 2 * blk : (a + 1) * 2 * blk, :].astype(BF16)


def grads_kernel(blk, n_back, core_ref, e_ref, inv_ref, dot_ref, q_own, q_other, *refs):
    n_arr = n_back + 1
    k_refs = refs[:n_arr]
    v_refs = refs[n_arr : 2 * n_arr]
    out_ref, dq_ref, other_ref = refs[2 * n_arr : 2 * n_arr + 3]
    dk_refs = refs[2 * n_arr + 3 : 3 * n_arr + 3]
    dk_acc, q_buf, out_buf, dq_buf = refs[3 * n_arr + 3 :]
    span_blocks = WINDOW // blk + 1
    core = core_ref[0]

    q_buf[core] = q_own[...]
    q_buf[1 - core] = q_other[...]

    def block_of(arrays, j):
        return arrays[j // 2][(j % 2) * blk : (j % 2 + 1) * blk, :]

    for qb in range(2):
        qs = jnp.concatenate([q_buf[qb, :, r * HD : (r + 1) * HD] for r in range(GROUP)], 0)
        do_t = dot_ref[0, qb]
        out_t = None
        for j in range(span_blocks):
            e = e_ref[0, qb, j * blk : (j + 1) * blk, :]
            part = dot(block_of(v_refs, qb + j), e, TN)
            out_t = part if out_t is None else out_t + part
        out_t = (out_t * inv_ref[0, qb]).astype(BF16).astype(F32)
        delta = jnp.sum(out_t * do_t.astype(F32), axis=0, keepdims=True)
        out = out_t.T.astype(BF16)
        dq_t = None
        for j in range(span_blocks):
            e = e_ref[0, qb, j * blk : (j + 1) * blk, :].astype(F32)
            dp = dot(block_of(v_refs, qb + j), do_t)
            ds = (e * (dp - delta)).astype(BF16)
            term = dot(ds, qs)
            at = slice((qb + j) * blk, (qb + j + 1) * blk)
            if qb == 0 or j == span_blocks - 1:
                dk_acc[at, :] = term
            else:
                dk_acc[at, :] += term
            part = dot(block_of(k_refs, qb + j), ds, TN)
            dq_t = part if dq_t is None else dq_t + part
        dq = (dq_t * score_scale).T.astype(BF16)
        for r in range(GROUP):
            out_buf[qb, :, r * HD : (r + 1) * HD] = out[r * blk : (r + 1) * blk, :]
            dq_buf[qb, :, r * HD : (r + 1) * HD] = dq[r * blk : (r + 1) * blk, :]
    out_ref[...] = out_buf[core]
    dq_ref[...] = dq_buf[core]
    other_ref[0] = out_buf[1 - core]
    other_ref[1] = dq_buf[1 - core]
    for a in range(n_arr):
        dk_refs[a][...] = (dk_acc[a * 2 * blk : (a + 1) * 2 * blk, :] * score_scale).astype(BF16)


def specs_of(rows, width):
    blk = rows // 2
    heads = width // HD
    span = WINDOW + blk
    lanes = GROUP * blk
    head = pl.BlockSpec((rows, HD), lambda g, c: (0, g))
    own = pl.BlockSpec((blk, GROUP * HD), lambda g, c: (0, c[0] * heads + g))
    return blk, heads, span, lanes, head, own


def run_probs(core, low, q, q_other, do, keys, rows, width):
    blk, heads, span, lanes, head, own = specs_of(rows, width)
    n_arr = len(keys)
    return pl.pallas_call(
        functools.partial(probs_kernel, blk, n_arr - 1),
        grid_spec=pltpu.PrefetchScalarGridSpec(
            num_scalar_prefetch=1,
            grid=(heads,),
            in_specs=[
                pl.BlockSpec((1, rows), lambda g, c: (0, 0)),
                own,
                pl.BlockSpec((blk, GROUP * HD), lambda g, c: (0, g)),
                own,
                pl.BlockSpec((blk, GROUP * HD), lambda g, c: (0, heads + g)),
            ]
            + [head] * n_arr,
            out_specs=[
                pl.BlockSpec((1, 2, span, lanes), lambda g, c: (g, 0, 0, 0)),
                pl.BlockSpec((1, 2, 1, lanes), lambda g, c: (g, 0, 0, 0)),
                pl.BlockSpec((1, 2, HD, lanes), lambda g, c: (g, 0, 0, 0)),
            ]
            + [head] * n_arr,
            scratch_shapes=[
                pltpu.VMEM((2, span, blk), F32),
                pltpu.VMEM((span // blk, blk, lanes), F32),
                pltpu.VMEM((WINDOW + rows, HD), F32),
                pltpu.VMEM((2, blk, GROUP * HD), BF16),
                pltpu.VMEM((2, blk, GROUP * HD), BF16),
            ],
        ),
        out_shape=[
            jax.ShapeDtypeStruct((heads, 2, span, lanes), BF16),
            jax.ShapeDtypeStruct((heads, 2, 1, lanes), F32),
            jax.ShapeDtypeStruct((heads, 2, HD, lanes), BF16),
        ]
        + [jax.ShapeDtypeStruct((rows, width), BF16)] * n_arr,
        compiler_params=pltpu.CompilerParams(vmem_limit_bytes=40 * 1024 * 1024),
        cost_estimate=pl.CostEstimate(
            flops=heads * 2 * span * lanes * HD * 2 * 2 * 6,
            bytes_accessed=heads * 2 * span * lanes * 2,
            transcendentals=0,
        ),
        name="probs",
    )(core, low, q, q_other, do, q_other, *keys)


def run_grads(core, e, inv, do_t, q, q_other, keys, values, rows, width):
    blk, heads, span, lanes, head, own = specs_of(rows, width)
    n_arr = len(keys)
    full = jax.ShapeDtypeStruct(q.shape, BF16)
    return pl.pallas_call(
        functools.partial(grads_kernel, blk, n_arr - 1),
        grid_spec=pltpu.PrefetchScalarGridSpec(
            num_scalar_prefetch=1,
            grid=(heads,),
            in_specs=[
                pl.BlockSpec((1, 2, span, lanes), lambda g, c: (g, 0, 0, 0)),
                pl.BlockSpec((1, 2, 1, lanes), lambda g, c: (g, 0, 0, 0)),
                pl.BlockSpec((1, 2, HD, lanes), lambda g, c: (g, 0, 0, 0)),
                own,
                pl.BlockSpec((blk, GROUP * HD), lambda g, c: (0, g)),
            ]
            + [head] * (2 * n_arr),
            out_specs=[own, own, pl.BlockSpec((2, blk, GROUP * HD), lambda g, c: (0, 0, g))] + [head] * n_arr,
            scratch_shapes=[
                pltpu.VMEM((WINDOW + rows, HD), F32),
                pltpu.VMEM((2, blk, GROUP * HD), BF16),
                pltpu.VMEM((2, blk, GROUP * HD), BF16),
                pltpu.VMEM((2, blk, GROUP * HD), BF16),
            ],
        ),
        out_shape=[full, full, jax.ShapeDtypeStruct((2, blk, GROUP * width), BF16)]
        + [jax.ShapeDtypeStruct((rows, width), BF16)] * n_arr,
        compiler_params=pltpu.CompilerParams(vmem_limit_bytes=40 * 1024 * 1024),
        cost_estimate=pl.CostEstimate(
            flops=heads * 2 * span * lanes * HD * 2 * 4 * 4,
            bytes_accessed=heads * 2 * span * lanes * 2,
            transcendentals=0,
        ),
        name="grads",
    )(core, e, inv, do_t, q, q_other, *keys, *values)


def shifted(x, by):
    length = lax.axis_size("ctx")
    return lax.ppermute(x, "ctx", [(i, i + by) for i in range(length) if 0 <= i + by < length])


def swapped(x):
    return lax.ppermute(x, "ctx", [(i, i ^ 1) for i in range(lax.axis_size("ctx"))])


def rotated(x, by):
    length = lax.axis_size("fsdp")
    return lax.ppermute(x, "fsdp", [(i, (i + by) % length) for i in range(length)])


def moved(x, flip, by):
    n_ctx, n_fsdp = lax.axis_size("ctx"), lax.axis_size("fsdp")
    pairs = [
        (c * n_fsdp + f, (c ^ (2 * flip)) * n_fsdp + (f + by) % n_fsdp)
        for c in range(n_ctx)
        for f in range(n_fsdp)
    ]
    return lax.ppermute(x, ("ctx", "fsdp"), pairs)


def cols(x, at, width):
    return lax.dynamic_slice_in_dim(x, at * width, width, x.ndim - 1)


def rows_of(x, at, count):
    return lax.dynamic_slice_in_dim(x, at * count, count, 0)


def placed(core, own, other, axis):
    both = jnp.concatenate([own, own], axis)
    return lax.dynamic_update_slice_in_dim(both, other, (1 - core) * own.shape[axis], axis)


def shards(hidden, queries, key_heads, w_value, d_out, segments):
    shard_rows = hidden.shape[1]
    model = hidden.shape[2]
    kv_width = w_value.shape[1]
    n_ctx = lax.axis_size("ctx")
    n_fsdp = lax.axis_size("fsdp")
    chip_rows = 2 * shard_rows
    n_back = WINDOW // chip_rows
    n_z = n_ctx // 4
    my_ctx = lax.axis_index("ctx")
    my_fsdp = lax.axis_index("fsdp")
    core = my_ctx % 2
    core_arg = core.astype(jnp.int32).reshape(1)
    chip = my_ctx // 2
    my_y = chip % 2
    my_z = chip // 2
    half_kv = kv_width // 2
    slab = model // n_fsdp
    tokens = hidden[0]
    first = chip * chip_rows

    sent = [rotated(cols(tokens, (my_fsdp + s) % n_fsdp, slab), s) for s in range(1, n_fsdp)]

    own_tags = segments[0].astype(BF16)
    tag_row = lax.dynamic_update_slice_in_dim(jnp.zeros((half_kv,), BF16), own_tags, core * shard_rows, 0)
    tag_rows = jnp.concatenate([tag_row[None], jnp.zeros((15, half_kv), BF16)], 0)
    got = swapped(jnp.concatenate([cols(key_heads[0], 1 - core, half_kv), tag_rows], 0))
    k_own = jnp.concatenate(
        [
            placed(core, cols(key_heads[0], core, half_kv), got[:shard_rows], 0),
            tag_rows + got[shard_rows:],
        ],
        0,
    )
    keys = [shifted(k_own, 2 * d) for d in range(n_back, 0, -1)] + [k_own]
    half_q = queries.shape[2] // 2
    q_other = swapped(jnp.concatenate([cols(queries[0], 1 - core, half_q), cols(d_out[0], 1 - core, half_q)], 1))

    out_rows = model // (n_ctx * n_fsdp)
    by_place = tokens.T.reshape(n_z, 2, 2, n_fsdp, out_rows, shard_rows)

    def rows_for(y, f):
        piece = lax.dynamic_index_in_dim(by_place, y, 1, keepdims=False)
        piece = lax.dynamic_index_in_dim(piece, f, 2, keepdims=False)
        return piece.reshape(n_z * 2 * out_rows, shard_rows)

    places = [(flip, s) for flip in range(2) for s in range(n_fsdp)]
    pieces = []
    for flip, s in places:
        piece = rows_for(my_y ^ flip, (my_fsdp + s) % n_fsdp)
        pieces.append(moved(piece, flip, s) if flip or s else piece)
    mine = jnp.concatenate(pieces, 1)
    theirs = swapped(mine)

    span_tags = jnp.concatenate([k[chip_rows, :chip_rows] for k in keys], 0)
    key_at = jnp.arange(WINDOW + chip_rows, dtype=jnp.int32)
    chip_tags = keys[n_back][chip_rows, :chip_rows]
    before = (span_tags[None, :] < chip_tags[:, None]) | (key_at + first < WINDOW)[None, :]
    low = jnp.sum(before.astype(jnp.int32), axis=1)
    low = jnp.maximum(low, jnp.arange(1, chip_rows + 1, dtype=jnp.int32))[None, :]

    e, inv, do_t, *dv_terms = run_probs(
        core_arg, low, queries[0], q_other, d_out[0], keys, chip_rows, half_kv
    )
    dv_total = dv_terms[n_back].astype(F32)
    for d in range(1, n_back + 1):
        dv_total = dv_total + shifted(dv_terms[n_back - d], -2 * d).astype(F32)
    dv_chip = dv_total.astype(BF16)

    value_sum = dot(cols(tokens, my_fsdp, slab), w_value)
    for s in range(1, n_fsdp):
        back = rotated(dot(sent[s - 1], w_value).astype(BF16), -s)
        value_sum = value_sum + back.astype(F32)
    own_values = value_sum.astype(BF16)
    v_own = placed(core, cols(own_values, core, half_kv), swapped(cols(own_values, 1 - core, half_kv)), 0)
    vals = [shifted(v_own, 2 * d) for d in range(n_back, 0, -1)] + [v_own]

    dv_places = [moved(dv_chip, flip, s) if flip or s else dv_chip for flip, s in places]
    weight_term = None
    for at, dv_of in enumerate(dv_places):
        window = slice(at * shard_rows, (at + 1) * shard_rows)
        term = dot(mine[:, window], rows_of(dv_of, core, shard_rows))
        term = term + dot(theirs[:, window], rows_of(dv_of, 1 - core, shard_rows))
        weight_term = term if weight_term is None else weight_term + term
    by_z = weight_term.astype(BF16).reshape(n_z, 2 * out_rows, half_kv)
    row_sum = lax.dynamic_index_in_dim(by_z, my_z, 0, keepdims=False).astype(F32)
    for d in range(1, n_z):
        piece = lax.dynamic_index_in_dim(by_z, (my_z + d) % n_z, 0, keepdims=False)
        piece = lax.ppermute(piece, "ctx", [(i, (i + 4 * d) % n_ctx) for i in range(n_ctx)])
        row_sum = row_sum + piece.astype(F32)
    d_weight = placed(core, rows_of(row_sum, core, out_rows), swapped(rows_of(row_sum, 1 - core, out_rows)), 1)

    dv_fsdp = [dv_places[s] for s in range(n_fsdp)]
    dv_other = swapped(jnp.concatenate([rows_of(x, 1 - core, shard_rows) for x in dv_fsdp], 0))
    dv_rows = placed(
        core, jnp.concatenate([rows_of(x, core, shard_rows) for x in dv_fsdp], 0), dv_other, 1
    )
    made = dot(dv_rows, w_value, NT).astype(BF16)
    d_tokens = jnp.concatenate([made[:shard_rows]] * n_fsdp, 1)
    for s in range(1, n_fsdp):
        back = rotated(made[s * shard_rows : (s + 1) * shard_rows], -s)
        d_tokens = lax.dynamic_update_slice_in_dim(d_tokens, back, ((my_fsdp + s) % n_fsdp) * slab, 1)

    out, dq, other, *dk_terms = run_grads(
        core_arg, e, inv, do_t, queries[0], q_other, keys, vals, chip_rows, half_kv
    )
    dk_total = dk_terms[n_back].astype(F32)
    for d in range(1, n_back + 1):
        dk_total = dk_total + shifted(dk_terms[n_back - d], -2 * d).astype(F32)
    dk_chip = dk_total.astype(BF16)
    d_keys = placed(core, rows_of(dk_chip, core, shard_rows), swapped(rows_of(dk_chip, 1 - core, shard_rows)), 1)
    other = swapped(other)
    out = lax.dynamic_update_slice_in_dim(out, other[0], (1 - core) * half_q, 1)
    dq = lax.dynamic_update_slice_in_dim(dq, other[1], (1 - core) * half_q, 1)
    return (out[None], dq[None], d_keys[None], d_tokens[None], d_weight)


def solution(mesh):
    in_specs = (
        P("fsdp", "ctx", None),
        P("fsdp", "ctx", None),
        P("fsdp", "ctx", None),
        P("fsdp", None),
        P("fsdp", "ctx", None),
        P("fsdp", "ctx"),
    )
    out_specs = (
        P("fsdp", "ctx", None),
        P("fsdp", "ctx", None),
        P("fsdp", "ctx", None),
        P("fsdp", "ctx", None),
        P(("ctx", "fsdp"), None),
    )
    return jax.shard_map(shards, mesh=mesh, in_specs=in_specs, out_specs=out_specs, check_vma=False)
```

time: 303 us -> 232 us (0.77)
  local copies, waits for them, and re-layouts: 33.9 us -> 12.9 us
  waiting for transfers between devices: 119 us -> 100 us
  blocking collectives: 18.7 us -> 0 us
  starting transfers between devices: 38.2 us -> 54.1 us
  between operations: 14.4 us -> 1.31 us
  other arithmetic: 17.7 us -> 7.92 us
  matrix products: 28.3 us -> 21.5 us
    ppermute x15 -> x20, waiting for transfers between devices: 119 us -> 98.3 us  [the longest x8 50.1 us: shifted(): lax.ppermute(x, 'ctx', [(i, i + by) for i in range(length) if 0 <= i + by...]
    all_gather x1 -> x0, blocking collectives: 18.7 us -> none  [shards(): tags = lax.all_gather(segments[0], 'ctx', axis=0, tiled=True)]
    dynamic_update_slice x3 -> x7, local copies, waits for them, and re-layouts: 16.5 us -> 0.46 us  [the longest x1 0.19 us: shards(): lax.dynamic_update_slice_in_dim(d_tokens, back, (my_fsdp + s) % n_fsdp *...]
    ppermute x15 -> x20, starting transfers between devices: 28.5 us -> 41.2 us  [the longest x8 27.8 us: shifted(): lax.ppermute(x, 'ctx', [(i, i + by) for i in range(length) if 0 <= i + by...]
    select_n x9 -> x0, other arithmetic: 12.6 us -> none  [pair(): jnp.where(core == 0, jnp.concatenate([own, other], axis), jnp.concatenate...]
    dot_general x6 -> x11, matrix products: 28.3 us -> 21.5 us  [dot(): return lax.dot_general(a, b, dims, preferred_element_type=F32)]
    concatenate x0 -> x10, other arithmetic: none -> 4.44 us  [the longest x1 2.26 us: shards(): mine = jnp.concatenate(pieces, 1)]
    dynamic_slice x6 -> x4, local copies, waits for them, and re-layouts: 7.45 us -> 3.57 us  [cols(): return lax.dynamic_slice_in_dim(x, at * width, width, x.ndim - 1)]
  transfers between devices with their start and end apart: 27 -> 28, of which waited for: 11 -> 15; matrix products, arithmetic and copies ran while one was open for 22% -> 17% of each run, Pallas kernels for 10% -> 13%
where the time goes in v2:
time: 232 us; the launch traced here: 228 us
  waiting for transfers between devices  100 us (43%)
  starting transfers between devices  54.1 us (23%)
  Pallas kernels  30.3 us (13%)
  matrix products  21.5 us (9%)
  local copies, waits for them, and re-layouts  12.9 us (6%)
  other arithmetic  7.92 us (3%)
    ppermute x8, waiting for transfers between devices, shifted(): lax.ppermute(x, 'ctx', [(i, i + by) for i in range(length) if 0 <= i + by...  50.1 us
    ppermute x3, waiting for transfers between devices, shards(): lax.ppermute(piece, 'ctx', [(i, (i + 4 * d) % n_ctx) for i in range(n_ctx)])  28.3 us
    ppermute x8, starting transfers between devices, shifted(): lax.ppermute(x, 'ctx', [(i, i + by) for i in range(length) if 0 <= i + by...  27.8 us
    dot_general x11, matrix products, dot(): return lax.dot_general(a, b, dims, preferred_element_type=F32)  21.5 us
    pallas_call x1, Pallas kernels, run_grads(): pl.pallas_call(functools.partial(grads_kernel, blk, n_arr - 1), grid_spec...  15.8 us
    pallas_call x1, Pallas kernels, run_probs(): pl.pallas_call(functools.partial(probs_kernel, blk, n_arr - 1), grid_spec...  14.5 us
    ppermute x8, starting transfers between devices, swapped(): lax.ppermute(x, 'ctx', [(i, i ^ 1) for i in range(lax.axis_size('ctx'))])  12.9 us
    ppermute x6, waiting for transfers between devices, moved(): return lax.ppermute(x, ('ctx', 'fsdp'), pairs)  12.1 us
  transfers between devices with their start and end apart: 28, of which 15 were waited for; matrix products, arithmetic and copies ran while one was open for 17% of the time, Pallas kernels for 13%

profile of v2, /device:TPU:9, one launch (start us, length us, event | category | flops | bytes accessed | tf_op | source)
XLA Modules:
  0.0 228.5 jit_solution(13518385930032663284)
XLA Ops:
  1.4 1.1 dynamic-slice_bitcast_fusion.7
  4.0 1.3 dynamic-slice_bitcast_fusion.1
  6.5 3.1 %collective-permute-start.2 = (bf16[528,512]{1,0:T(8,128)(2,1)S(1)}, bf16[528,512]{1,0:T(8,128)(2,1)}, u32[]{:S(2)}, u32[]{:S(2)}) collective-permute-start(bf16[528,512]{1,0:T(8,128)(2,1)S(1)} %pad_maximum_fusion.3.refs_2_), channel_id=1, source_target_pairs={{0,4},{2,6},{4,8},{6,10},{8,12},{10,14},{12,16},{14,18},{16,20},{1... | collective-permute-start | bytes 1622024 | tf_op jit(solution)/shard_map/ppermute | solution.py:239
  9.7 3.2 %collective-permute-start.1 = (bf16[528,512]{1,0:T(8,128)(2,1)S(1)}, bf16[528,512]{1,0:T(8,128)(2,1)}, u32[]{:S(2)}, u32[]{:S(2)}) collective-permute-start(bf16[528,512]{1,0:T(8,128)(2,1)S(1)} %pad_maximum_fusion.3.refs_2_), channel_id=1, source_target_pairs={{0,8},{2,10},{4,12},{6,14},{8,16},{10,18},{12,20},{14,22},{16,24},... | collective-permute-start | bytes 1622024 | tf_op jit(solution)/shard_map/ppermute | solution.py:239
  12.9 1.2 dynamic-slice_bitcast_fusion
  14.1 1.2 collective-permute-start.4
  15.3 4.6 %copy.12 = bf16[1,256,5376]{1,2,0:T(8,128)(2,1)} copy(bf16[1,256,5376]{2,1,0:T(8,128)(2,1)} %param.6) | data formatting | bytes 5505024 | tf_op args[0]
  20.0 2.8 %collective-permute-done.2.refs_1_ = bf16[528,512]{1,0:T(8,128)(2,1)} collective-permute-done((bf16[528,512]{1,0:T(8,128)(2,1)S(1)}, bf16[528,512]{1,0:T(8,128)(2,1)}, u32[]{:S(2)}, u32[]{:S(2)}) %collective-permute-start.2) | collective-permute-done | bytes 540704 | tf_op jit(solution)/shard_map/ppermute | solution.py:239
  23.4 1.2 collective-permute-done.1.refs_0_
  26.1 14.5 %probs.1 = (bf16[4,2,1280,512]{3,2,1,0:T(8,128)(2,1)}, f32[4,2,1,512]{3,2,1,0:T(1,128)S(1)}, bf16[4,2,128,512]{3,2,1,0:T(8,128)(2,1)S(1)}, bf16[512,512]{1,0:T(8...) custom-call(s32[1]{0:T(128)} %bitcast.core_ref, s32[1,512]{1,0:T(1,128)S(1)} %add_maximum_fusion.low_ref, ...), custom_call_target="tpu_custom_call" | custom-call | flops 16106127360 | bytes 10485760 | tf_op jit(solution)/shard_map/probs/pallas_call | solution.py:157
  40.6 1.9 collective-permute-start.14
  42.5 10.1 %collective-permute-start.13 = (bf16[512,512]{1,0:T(8,128)(2,1)}, bf16[512,512]{1,0:T(8,128)(2,1)}, u32[]{:S(2)}, u32[]{:S(2)}) collective-permute-start(bf16[512,512]{1,0:T(8,128)(2,1)} %get-tuple-element.27), channel_id=1, source_target_pairs={{4,0},{6,2},{8,4},{10,6},{12,8},{14,10},{16,12},{18,14},{20,16},{2... | collective-permute-start | bytes 1572872 | tf_op jit(solution)/shard_map/ppermute | solution.py:239
  52.6 1.4 constant_dynamic-slice_fusion.5
  54.0 2.7 %collective-permute-start.20 = (bf16[1344,256]{1,0:T(8,128)(2,1)}, bf16[1344,256]{1,0:T(8,128)(2,1)}, u32[]{:S(2)}, u32[]{:S(2)}) collective-permute-start(bf16[1344,256]{1,0:T(8,128)(2,1)} %bitcast.24), channel_id=1, source_target_pairs={{0,5},{1,4},{2,7},{3,6},{4,1},{5,0},{6,3},{7,2},{8,13},{9,12},{10,... | collective-permute-start | bytes 2064392 | tf_op jit(solution)/shard_map/ppermute | solution.py:258
  56.7 4.7 %fusion.4 = f32[256,1024]{1,0:T(8,128)S(1)} fusion(bf16[2688,1024]{1,0:T(8,128)(2,1)} %param.9, bf16[1,256,5376]{2,1,0:T(8,128)(2,1)} %param.6, s32[]{:T(128)S(6)} %select_n.143), kind=kOutput, calls=%fused_computation.13 | convolution fusion | flops 1409286144 | bytes 7929860 | tf_op jit(solution)/shard_map/dot_general | solution.py:28
  61.7 18.5 %collective-permute-done.13 = bf16[512,512]{1,0:T(8,128)(2,1)} collective-permute-done((bf16[512,512]{1,0:T(8,128)(2,1)}, bf16[512,512]{1,0:T(8,128)(2,1)}, u32[]{:S(2)}, u32[]{:S(2)}) %collective-permute-start.13) | collective-permute-done | bytes 524320 | tf_op jit(solution)/shard_map/ppermute | solution.py:239
  80.3 1.4 add_convert_fusion
  81.7 1.3 collective-permute-start.15
  82.9 4.6 %convolution_convert_fusion.1 = bf16[256,1024]{1,0:T(8,128)(2,1)S(1)} fusion(bf16[256,2688]{1,0:T(8,128)(2,1)} %collective-permute-done.4, bf16[2688,1024]{1,0:T(8,128)(2,1)} %param.9), kind=kOutput, calls=%fused_computation.17 | convolution fusion | flops 1409548288 | bytes 7405568 | tf_op jit(solution)/shard_map/dot_general | solution.py:28
  87.9 8.8 %collective-permute-done.19 = bf16[1344,256]{1,0:T(8,128)(2,1)} collective-permute-done((bf16[1344,256]{1,0:T(8,128)(2,1)}, bf16[1344,256]{1,0:T(8,128)(2,1)}, u32[]{:S(2)}, u32[]{:S(2)}) %collective-permute-start.19) | collective-permute-done | bytes 688160 | tf_op jit(solution)/shard_map/ppermute | solution.py:258
  96.7 2.3 pad_maximum_fusion
  98.9 2.9 %collective-permute-start.21 = (bf16[1344,1024]{1,0:T(8,128)(2,1)S(1)}, bf16[1344,1024]{1,0:T(8,128)(2,1)S(1)}, u32[]{:S(2)}, u32[]{:S(2)}) collective-permute-start(bf16[1344,1024]{1,0:T(8,128)(2,1)S(1)} %pad_maximum_fusion), channel_id=1, source_target_pairs={{0,2},{2,0},{4,6},{6,4},{8,10},{10,8},{12,14},{14,12},{16,18},{18,... | collective-permute-start | bytes 8257544 | tf_op jit(solution)/shard_map/ppermute | solution.py:243
  102.7 1.6 collective-permute-start.22
  104.3 3.3 %collective-permute-done.15 = bf16[512,512]{1,0:T(8,128)(2,1)S(1)} collective-permute-done((bf16[512,512]{1,0:T(8,128)(2,1)S(1)}, bf16[512,512]{1,0:T(8,128)(2,1)S(1)}, u32[]{:S(2)}, u32[]{:S(2)}) %collective-permute-start.15) | collective-permute-done | bytes 524320 | tf_op jit(solution)/shard_map/ppermute | solution.py:258
  107.7 3.2 %collective-permute-start.16 = (bf16[512,512]{1,0:T(8,128)(2,1)S(1)}, bf16[512,512]{1,0:T(8,128)(2,1)S(1)}, u32[]{:S(2)}, u32[]{:S(2)}) collective-permute-start(bf16[512,512]{1,0:T(8,128)(2,1)S(1)} %pad_maximum_fusion.6), channel_id=1, source_target_pairs={{0,2},{2,0},{4,6},{6,4},{8,10},{10,8},{12,14},{14,12},{16,18},{18,... | collective-permute-start | bytes 1572872 | tf_op jit(solution)/shard_map/ppermute | solution.py:243
  111.0 7.9 %collective-permute-done.5 = bf16[256,1024]{1,0:T(8,128)(2,1)S(1)} collective-permute-done((bf16[256,1024]{1,0:T(8,128)(2,1)S(1)}, bf16[256,1024]{1,0:T(8,128)(2,1)S(1)}, u32[]{:S(2)}, u32[]{:S(2)}) %collective-permute-start.5) | collective-permute-done | bytes 524320 | tf_op jit(solution)/shard_map/ppermute | solution.py:248
  119.1 3.2 %collective-permute-start.6 = (bf16[256,512]{1,0:T(8,128)(2,1)S(1)}, bf16[256,512]{1,0:T(8,128)(2,1)S(1)}, u32[]{:S(2)}, u32[]{:S(2)}) collective-permute-start(bf16[256,512]{1,0:T(8,128)(2,1)S(1)} %get-tuple-element.48), channel_id=1, source_target_pairs={{0,2},{2,0},{4,6},{6,4},{8,10},{10,8},{12,14},{14,12},{16,18},{18,... | collective-permute-start | bytes 786440 | tf_op jit(solution)/shard_map/ppermute | solution.py:243
  123.5 3.5 %collective-permute-start.7 = (bf16[512,512]{1,0:T(8,128)(2,1)S(1)}, bf16[512,512]{1,0:T(8,128)(2,1)S(1)}, u32[]{:S(2)}, u32[]{:S(2)}) collective-permute-start(bf16[512,512]{1,0:T(8,128)(2,1)S(1)} %constant_dynamic-update-slice_fusion.2.refs_5_), channel_id=1, source_target_pairs={{0,8},{2,10},{4,12},{6,14},{8,16},{10,18},{12,20},{14,22},{16,24},... | collective-permute-start | bytes 1572872 | tf_op jit(solution)/shard_map/ppermute | solution.py:239
  127.1 2.1 collective-permute-start.8
  129.3 3.5 %convolution_convert_fusion = bf16[512,2688]{1,0:T(8,128)(2,1)S(1)} fusion(bf16[512,1024]{1,0:T(8,128)(2,1)S(1)} %constant_dynamic-update-slice_fusion.1, bf16[2688,1024]{1,0:T(8,128)(2,1)S(1)} %bitcast.70), kind=kOutput, calls=%fused_computation | convolution fusion | flops 2819948544 | bytes 9306112 | tf_op jit(solution)/shard_map/dot_general | solution.py:28
  133.0 5.6 %collective-permute-done.7.refs_3_ = bf16[512,512]{1,0:T(8,128)(2,1)S(1)} collective-permute-done((bf16[512,512]{1,0:T(8,128)(2,1)S(1)}, bf16[512,512]{1,0:T(8,128)(2,1)S(1)}, u32[]{:S(2)}, u32[]{:S(2)}) %collective-permute-start.7) | collective-permute-done | bytes 524320 | tf_op jit(solution)/shard_map/ppermute | solution.py:239
  138.5 4.1 %collective-permute-done.8.refs_4_ = bf16[512,512]{1,0:T(8,128)(2,1)S(1)} collective-permute-done((bf16[512,512]{1,0:T(8,128)(2,1)S(1)}, bf16[512,512]{1,0:T(8,128)(2,1)S(1)}, u32[]{:S(2)}, u32[]{:S(2)}) %collective-permute-start.8) | collective-permute-done | bytes 524320 | tf_op jit(solution)/shard_map/ppermute | solution.py:239
  142.7 15.8 %grads.1 = (bf16[256,2048]{1,0:T(8,128)(2,1)}, bf16[256,2048]{1,0:T(8,128)(2,1)}, bf16[2,256,1024]{2,1,0:T(8,128)(2,1)S(1)}, bf16[512,512]{1,0:T(8,128)(2,1)S(1)...) custom-call(s32[1]{0:T(128)} %bitcast.core_ref, bf16[4,2,1280,512]{3,2,1,0:T(8,128)(2,1)} %get-tuple-element.17.e_ref, ...), custom_call_target="tpu_custom_call" | custom-call | flops 21474836480 | bytes 10485760 | tf_op jit(solution)/shard_map/grads/pallas_call | solution.py:204
  158.5 1.9 collective-permute-start.11
  160.4 1.9 collective-permute-start.10
  162.5 9.7 %collective-permute-done.11 = bf16[512,512]{1,0:T(8,128)(2,1)S(1)} collective-permute-done((bf16[512,512]{1,0:T(8,128)(2,1)S(1)}, bf16[512,512]{1,0:T(8,128)(2,1)S(1)}, u32[]{:S(2)}, u32[]{:S(2)}) %collective-permute-start.11) | collective-permute-done | bytes 524320 | tf_op jit(solution)/shard_map/ppermute | solution.py:239
  172.3 1.2 collective-permute-start.17
  173.4 8.2 %collective-permute-done.10 = bf16[512,512]{1,0:T(8,128)(2,1)S(1)} collective-permute-done((bf16[512,512]{1,0:T(8,128)(2,1)S(1)}, bf16[512,512]{1,0:T(8,128)(2,1)S(1)}, u32[]{:S(2)}, u32[]{:S(2)}) %collective-permute-start.10) | collective-permute-done | bytes 524320 | tf_op jit(solution)/shard_map/ppermute | solution.py:239
  181.6 2.2 collective-permute-start.9
  185.2 1.5 fusion.7
  186.7 1.7 convolution_add_fusion
  189.6 1.5 fusion.9
  191.1 1.9 fusion.3
  193.1 2.6 %collective-permute-start.25 = (bf16[336,512]{1,0:T(8,128)(2,1)S(1)}, bf16[336,512]{1,0:T(8,128)(2,1)S(1)}, u32[]{:S(2)}, u32[]{:S(2)}) collective-permute-start(bf16[336,512]{1,0:T(8,128)(2,1)S(1)} %get-tuple-element.37), channel_id=1, source_target_pairs={{0,16},{2,18},{4,20},{6,22},{8,24},{10,26},{12,28},{14,30},{16,0},... | collective-permute-start | bytes 1032200 | tf_op jit(solution)/shard_map/ppermute | solution.py:362
  195.7 1.3 collective-permute-start.24
  197.2 5.0 %collective-permute-done.26 = bf16[336,512]{1,0:T(8,128)(2,1)S(1)} collective-permute-done((bf16[336,512]{1,0:T(8,128)(2,1)S(1)}, bf16[336,512]{1,0:T(8,128)(2,1)S(1)}, u32[]{:S(2)}, u32[]{:S(2)}) %collective-permute-start.26) | collective-permute-done | bytes 344096 | tf_op jit(solution)/shard_map/ppermute | solution.py:362
  202.2 15.9 %collective-permute-done.25 = bf16[336,512]{1,0:T(8,128)(2,1)S(1)} collective-permute-done((bf16[336,512]{1,0:T(8,128)(2,1)S(1)}, bf16[336,512]{1,0:T(8,128)(2,1)S(1)}, u32[]{:S(2)}, u32[]{:S(2)}) %collective-permute-start.25) | collective-permute-done | bytes 344096 | tf_op jit(solution)/shard_map/ppermute | solution.py:362
  218.1 7.4 %collective-permute-done.24 = bf16[336,512]{1,0:T(8,128)(2,1)S(1)} collective-permute-done((bf16[336,512]{1,0:T(8,128)(2,1)S(1)}, bf16[336,512]{1,0:T(8,128)(2,1)S(1)}, u32[]{:S(2)}, u32[]{:S(2)}) %collective-permute-start.24) | collective-permute-done | bytes 344096 | tf_op jit(solution)/shard_map/ppermute | solution.py:362
  (100 shorter events, 14.7 us)
Async XLA Ops:
  3.3 3.1 %collective-permute-start = (bf16[272,512]{1,0:T(8,128)(2,1)}, bf16[272,512]{1,0:T(8,128)(2,1)S(1)}, u32[]{:S(2)}, u32[]{:S(2)}) collective-permute-start(bf16[272,512]{1,0:T(8,128)(2,1)} %maximum_maximum_fusion.1), channel_id=1, source_target_pairs={{0,2},{2,0},{4,6},{6,4},{8,10},{10,8},{12,14},{14,12},{16,18},{18,... | collective-permute-start | bytes 835592 | tf_op jit(solution)/shard_map/ppermute | solution.py:243
  5.3 7.6 %copy-start.5 = (bf16[1,256,5376]{2,1,0:T(8,128)(2,1)S(1)}, bf16[1,256,5376]{2,1,0:T(8,128)(2,1)}, u32[]{:S(2)}) copy-start(bf16[1,256,5376]{2,1,0:T(8,128)(2,1)} %param.6) | copy-start | bytes 8257540
  6.4 19.7 %collective-permute-start.3 = (bf16[256,2048]{1,0:T(8,128)(2,1)}, bf16[256,2048]{1,0:T(8,128)(2,1)}, u32[]{:S(2)}, u32[]{:S(2)}) collective-permute-start(bf16[256,2048]{1,0:T(8,128)(2,1)} %pad_maximum_fusion.1), channel_id=1, source_target_pairs={{0,2},{2,0},{4,6},{6,4},{8,10},{10,8},{12,14},{14,12},{16,18},{18,... | collective-permute-start | bytes 3145736 | tf_op jit(solution)/shard_map/ppermute | solution.py:243
  6.5 16.2 %collective-permute-start.2 = (bf16[528,512]{1,0:T(8,128)(2,1)S(1)}, bf16[528,512]{1,0:T(8,128)(2,1)}, u32[]{:S(2)}, u32[]{:S(2)}) collective-permute-start(bf16[528,512]{1,0:T(8,128)(2,1)S(1)} %pad_maximum_fusion.3.refs_2_), channel_id=1, source_target_pairs={{0,4},{2,6},{4,8},{6,10},{8,12},{10,14},{12,16},{14,18},{16,20},{1... | collective-permute-start | bytes 1622024 | tf_op jit(solution)/shard_map/ppermute | solution.py:239
  9.7 15.0 %collective-permute-start.1 = (bf16[528,512]{1,0:T(8,128)(2,1)S(1)}, bf16[528,512]{1,0:T(8,128)(2,1)}, u32[]{:S(2)}, u32[]{:S(2)}) collective-permute-start(bf16[528,512]{1,0:T(8,128)(2,1)S(1)} %pad_maximum_fusion.3.refs_2_), channel_id=1, source_target_pairs={{0,8},{2,10},{4,12},{6,14},{8,16},{10,18},{12,20},{14,22},{16,24},... | collective-permute-start | bytes 1622024 | tf_op jit(solution)/shard_map/ppermute | solution.py:239
  14.1 68.9 %collective-permute-start.4 = (bf16[256,2688]{1,0:T(8,128)(2,1)}, bf16[256,2688]{1,0:T(8,128)(2,1)}, u32[]{:S(2)}, u32[]{:S(2)}) collective-permute-start(bf16[256,2688]{1,0:T(8,128)(2,1)} %dynamic-slice_bitcast_fusion), channel_id=1, source_target_pairs={{0,1},{1,0},{2,3},{3,2},{4,5},{5,4},{6,7},{7,6},{8,9},{9,8},{10,11... | collective-permute-start | bytes 4128776 | tf_op jit(solution)/shard_map/ppermute | solution.py:248
  15.3 10.7 %copy-start = (bf16[1,256,2048]{2,1,0:T(8,128)(2,1)S(1)}, bf16[1,256,2048]{2,1,0:T(8,128)(2,1)}, u32[]{:S(2)}) copy-start(bf16[1,256,2048]{2,1,0:T(8,128)(2,1)} %param.10) | copy-start | bytes 3145732
  15.3 10.8 %copy-start.1 = (bf16[1,256,2048]{2,1,0:T(8,128)(2,1)S(1)}, bf16[1,256,2048]{2,1,0:T(8,128)(2,1)}, u32[]{:S(2)}) copy-start(bf16[1,256,2048]{2,1,0:T(8,128)(2,1)} %param.7) | copy-start | bytes 3145732
  26.1 26.5 %copy-start.4 = (bf16[1,256,5376]{1,2,0:T(8,128)(2,1)S(1)}, bf16[1,256,5376]{1,2,0:T(8,128)(2,1)}, u32[]{:S(2)}) copy-start(bf16[1,256,5376]{1,2,0:T(8,128)(2,1)} %copy.12) | copy-start | bytes 8257540
  40.6 13.4 %copy-start.2 = (bf16[4,2,128,512]{3,2,1,0:T(8,128)(2,1)}, bf16[4,2,128,512]{3,2,1,0:T(8,128)(2,1)S(1)}, u32[]{:S(2)}) copy-start(bf16[4,2,128,512]{3,2,1,0:T(8,128)(2,1)S(1)} %get-tuple-element.19.dot_ref) | copy-start | bytes 3145732
  40.6 20.8 %collective-permute-start.14 = (bf16[512,512]{1,0:T(8,128)(2,1)}, bf16[512,512]{1,0:T(8,128)(2,1)}, u32[]{:S(2)}, u32[]{:S(2)}) collective-permute-start(bf16[512,512]{1,0:T(8,128)(2,1)} %get-tuple-element.28), channel_id=1, source_target_pairs={{8,0},{10,2},{12,4},{14,6},{16,8},{18,10},{20,12},{22,14},{24,16},... | collective-permute-start | bytes 1572872 | tf_op jit(solution)/shard_map/ppermute | solution.py:239
  42.5 37.7 %collective-permute-start.13 = (bf16[512,512]{1,0:T(8,128)(2,1)}, bf16[512,512]{1,0:T(8,128)(2,1)}, u32[]{:S(2)}, u32[]{:S(2)}) collective-permute-start(bf16[512,512]{1,0:T(8,128)(2,1)} %get-tuple-element.27), channel_id=1, source_target_pairs={{4,0},{6,2},{8,4},{10,6},{12,8},{14,10},{16,12},{18,14},{20,16},{2... | collective-permute-start | bytes 1572872 | tf_op jit(solution)/shard_map/ppermute | solution.py:239
  54.0 33.9 %collective-permute-start.20 = (bf16[1344,256]{1,0:T(8,128)(2,1)}, bf16[1344,256]{1,0:T(8,128)(2,1)}, u32[]{:S(2)}, u32[]{:S(2)}) collective-permute-start(bf16[1344,256]{1,0:T(8,128)(2,1)} %bitcast.24), channel_id=1, source_target_pairs={{0,5},{1,4},{2,7},{3,6},{4,1},{5,0},{6,3},{7,2},{8,13},{9,12},{10,... | collective-permute-start | bytes 2064392 | tf_op jit(solution)/shard_map/ppermute | solution.py:258
  56.7 40.0 %collective-permute-start.19 = (bf16[1344,256]{1,0:T(8,128)(2,1)}, bf16[1344,256]{1,0:T(8,128)(2,1)}, u32[]{:S(2)}, u32[]{:S(2)}) collective-permute-start(bf16[1344,256]{1,0:T(8,128)(2,1)} %bitcast.23), channel_id=1, source_target_pairs={{0,4},{1,5},{2,6},{3,7},{4,0},{5,1},{6,2},{7,3},{8,12},{9,13},{10,... | collective-permute-start | bytes 2064392 | tf_op jit(solution)/shard_map/ppermute | solution.py:258
  56.7 4.7 %copy-start.7 = (bf16[4,1,2,1,168,256]{5,4,3,2,1,0:T(8,128)(2,1)S(1)}, bf16[4,1,2,1,168,256]{5,4,3,2,1,0:T(8,128)(2,1)}, u32[]{:S(2)}) copy-start(bf16[4,1,2,1,168,256]{5,4,3,2,1,0:T(8,128)(2,1)} %get-tuple-element.32) | copy-start | bytes 2064388
  61.4 35.3 %collective-permute-start.18 = (bf16[1344,256]{1,0:T(8,128)(2,1)S(1)}, bf16[1344,256]{1,0:T(8,128)(2,1)S(1)}, u32[]{:S(2)}, u32[]{:S(2)}) collective-permute-start(bf16[1344,256]{1,0:T(8,128)(2,1)S(1)} %bitcast.67), channel_id=1, source_target_pairs={{0,1},{1,0},{2,3},{3,2},{4,5},{5,4},{6,7},{7,6},{8,9},{9,8},{10,11... | collective-permute-start | bytes 2064392 | tf_op jit(solution)/shard_map/ppermute | solution.py:258
  81.7 26.0 %collective-permute-start.15 = (bf16[512,512]{1,0:T(8,128)(2,1)S(1)}, bf16[512,512]{1,0:T(8,128)(2,1)S(1)}, u32[]{:S(2)}, u32[]{:S(2)}) collective-permute-start(bf16[512,512]{1,0:T(8,128)(2,1)S(1)} %add_convert_fusion), channel_id=1, source_target_pairs={{0,1},{1,0},{2,3},{3,2},{4,5},{5,4},{6,7},{7,6},{8,9},{9,8},{10,11... | collective-permute-start | bytes 1572872 | tf_op jit(solution)/shard_map/ppermute | solution.py:258
  87.6 31.3 %collective-permute-start.5 = (bf16[256,1024]{1,0:T(8,128)(2,1)S(1)}, bf16[256,1024]{1,0:T(8,128)(2,1)S(1)}, u32[]{:S(2)}, u32[]{:S(2)}) collective-permute-start(bf16[256,1024]{1,0:T(8,128)(2,1)S(1)} %convolution_convert_fusion.1), channel_id=1, source_target_pairs={{0,1},{1,0},{2,3},{3,2},{4,5},{5,4},{6,7},{7,6},{8,9},{9,8},{10,11... | collective-permute-start | bytes 1572872 | tf_op jit(solution)/shard_map/ppermute | solution.py:248
  96.7 32.6 %slice-start = ((s8[5505024]{0:T(1024)(128)(4,1)}), s8[4194304]{0:T(1024)(128)(4,1)S(1)}, s32[]{:S(2)}) async-start(s8[5505024]{0:T(1024)(128)(4,1)} %bitcast.69), calls=%async_computation | async-start | bytes 8388608
  98.9 85.2 %collective-permute-start.21 = (bf16[1344,1024]{1,0:T(8,128)(2,1)S(1)}, bf16[1344,1024]{1,0:T(8,128)(2,1)S(1)}, u32[]{:S(2)}, u32[]{:S(2)}) collective-permute-start(bf16[1344,1024]{1,0:T(8,128)(2,1)S(1)} %pad_maximum_fusion), channel_id=1, source_target_pairs={{0,2},{2,0},{4,6},{6,4},{8,10},{10,8},{12,14},{14,12},{16,18},{18,... | collective-permute-start | bytes 8257544 | tf_op jit(solution)/shard_map/ppermute | solution.py:243
  101.9 83.4 %collective-permute-start.23 = (bf16[512,512]{1,0:T(8,128)(2,1)S(1)}, bf16[512,512]{1,0:T(8,128)(2,1)}, u32[]{:S(2)}, u32[]{:S(2)}) collective-permute-start(bf16[512,512]{1,0:T(8,128)(2,1)S(1)} %add_convert_fusion), channel_id=1, source_target_pairs={{0,5},{1,4},{2,7},{3,6},{4,1},{5,0},{6,3},{7,2},{8,13},{9,12},{10,... | collective-permute-start | bytes 1572872 | tf_op jit(solution)/shard_map/ppermute | solution.py:258
  102.7 86.9 %collective-permute-start.22 = (bf16[512,512]{1,0:T(8,128)(2,1)S(1)}, bf16[512,512]{1,0:T(8,128)(2,1)}, u32[]{:S(2)}, u32[]{:S(2)}) collective-permute-start(bf16[512,512]{1,0:T(8,128)(2,1)S(1)} %add_convert_fusion), channel_id=1, source_target_pairs={{0,4},{1,5},{2,6},{3,7},{4,0},{5,1},{6,2},{7,3},{8,12},{9,13},{10,... | collective-permute-start | bytes 1572872 | tf_op jit(solution)/shard_map/ppermute | solution.py:258
  107.7 21.6 %slice-start.1 = ((s8[5505024]{0:T(1024)(128)(4,1)}), s8[1310720]{0:T(1024)(128)(4,1)S(1)}, s32[]{:S(2)}) async-start(s8[5505024]{0:T(1024)(128)(4,1)} %bitcast.69), calls=%async_computation.1 | async-start | bytes 2621440
  107.7 19.3 %collective-permute-start.16 = (bf16[512,512]{1,0:T(8,128)(2,1)S(1)}, bf16[512,512]{1,0:T(8,128)(2,1)S(1)}, u32[]{:S(2)}, u32[]{:S(2)}) collective-permute-start(bf16[512,512]{1,0:T(8,128)(2,1)S(1)} %pad_maximum_fusion.6), channel_id=1, source_target_pairs={{0,2},{2,0},{4,6},{6,4},{8,10},{10,8},{12,14},{14,12},{16,18},{18,... | collective-permute-start | bytes 1572872 | tf_op jit(solution)/shard_map/ppermute | solution.py:243
  119.1 4.4 %collective-permute-start.6 = (bf16[256,512]{1,0:T(8,128)(2,1)S(1)}, bf16[256,512]{1,0:T(8,128)(2,1)S(1)}, u32[]{:S(2)}, u32[]{:S(2)}) collective-permute-start(bf16[256,512]{1,0:T(8,128)(2,1)S(1)} %get-tuple-element.48), channel_id=1, source_target_pairs={{0,2},{2,0},{4,6},{6,4},{8,10},{10,8},{12,14},{14,12},{16,18},{18,... | collective-permute-start | bytes 786440 | tf_op jit(solution)/shard_map/ppermute | solution.py:243
  123.5 15.0 %collective-permute-start.7 = (bf16[512,512]{1,0:T(8,128)(2,1)S(1)}, bf16[512,512]{1,0:T(8,128)(2,1)S(1)}, u32[]{:S(2)}, u32[]{:S(2)}) collective-permute-start(bf16[512,512]{1,0:T(8,128)(2,1)S(1)} %constant_dynamic-update-slice_fusion.2.refs_5_), channel_id=1, source_target_pairs={{0,8},{2,10},{4,12},{6,14},{8,16},{10,18},{12,20},{14,22},{16,24},... | collective-permute-start | bytes 1572872 | tf_op jit(solution)/shard_map/ppermute | solution.py:239
  127.1 15.6 %collective-permute-start.8 = (bf16[512,512]{1,0:T(8,128)(2,1)S(1)}, bf16[512,512]{1,0:T(8,128)(2,1)S(1)}, u32[]{:S(2)}, u32[]{:S(2)}) collective-permute-start(bf16[512,512]{1,0:T(8,128)(2,1)S(1)} %constant_dynamic-update-slice_fusion.2.refs_5_), channel_id=1, source_target_pairs={{0,4},{2,6},{4,8},{6,10},{8,12},{10,14},{12,16},{14,18},{16,20},{1... | collective-permute-start | bytes 1572872 | tf_op jit(solution)/shard_map/ppermute | solution.py:239
  132.8 9.9 %copy-start.3 = (bf16[4,2,128,512]{3,2,1,0:T(8,128)(2,1)S(1)}, bf16[4,2,128,512]{3,2,1,0:T(8,128)(2,1)}, u32[]{:S(2)}) copy-start(bf16[4,2,128,512]{3,2,1,0:T(8,128)(2,1)} %copy-done.2) | copy-start | bytes 3145732
  158.5 13.7 %collective-permute-start.11 = (bf16[512,512]{1,0:T(8,128)(2,1)S(1)}, bf16[512,512]{1,0:T(8,128)(2,1)S(1)}, u32[]{:S(2)}, u32[]{:S(2)}) collective-permute-start(bf16[512,512]{1,0:T(8,128)(2,1)S(1)} %get-tuple-element.25), channel_id=1, source_target_pairs={{8,0},{10,2},{12,4},{14,6},{16,8},{18,10},{20,12},{22,14},{24,16},... | collective-permute-start | bytes 1572872 | tf_op jit(solution)/shard_map/ppermute | solution.py:239
  160.4 21.2 %collective-permute-start.10 = (bf16[512,512]{1,0:T(8,128)(2,1)S(1)}, bf16[512,512]{1,0:T(8,128)(2,1)S(1)}, u32[]{:S(2)}, u32[]{:S(2)}) collective-permute-start(bf16[512,512]{1,0:T(8,128)(2,1)S(1)} %get-tuple-element.24), channel_id=1, source_target_pairs={{4,0},{6,2},{8,4},{10,6},{12,8},{14,10},{16,12},{18,14},{20,16},{2... | collective-permute-start | bytes 1572872 | tf_op jit(solution)/shard_map/ppermute | solution.py:239
  172.3 54.1 %collective-permute-start.17 = (bf16[256,2688]{1,0:T(8,128)(2,1)S(1)}, bf16[256,2688]{1,0:T(8,128)(2,1)S(1)}, u32[]{:S(2)}, u32[]{:S(2)}) collective-permute-start(bf16[256,2688]{1,0:T(8,128)(2,1)S(1)} %get-tuple-element.33), channel_id=1, source_target_pairs={{0,1},{1,0},{2,3},{3,2},{4,5},{5,4},{6,7},{7,6},{8,9},{9,8},{10,11... | collective-permute-start | bytes 4128776 | tf_op jit(solution)/shard_map/ppermute | solution.py:248
  181.6 15.5 %collective-permute-start.9 = (bf16[2,256,1024]{2,1,0:T(8,128)(2,1)S(1)}, bf16[2,256,1024]{2,1,0:T(8,128)(2,1)S(1)}, u32[]{:S(2)}, u32[]{:S(2)}) collective-permute-start(bf16[2,256,1024]{2,1,0:T(8,128)(2,1)S(1)} %get-tuple-element.21), channel_id=1, source_target_pairs={{0,2},{2,0},{4,6},{6,4},{8,10},{10,8},{12,14},{14,12},{16,18},{18,... | collective-permute-start | bytes 3145736 | tf_op jit(solution)/shard_map/ppermute | solution.py:243
  184.1 11.7 %collective-permute-start.12 = (bf16[256,512]{1,0:T(8,128)(2,1)S(1)}, bf16[256,512]{1,0:T(8,128)(2,1)S(1)}, u32[]{:S(2)}, u32[]{:S(2)}) collective-permute-start(bf16[256,512]{1,0:T(8,128)(2,1)S(1)} %get-tuple-element.46), channel_id=1, source_target_pairs={{0,2},{2,0},{4,6},{6,4},{8,10},{10,8},{12,14},{14,12},{16,18},{18,... | collective-permute-start | bytes 786440 | tf_op jit(solution)/shard_map/ppermute | solution.py:243
  191.0 6.0 %copy-start.10 = (bf16[256,2048]{1,0:T(8,128)(2,1)S(1)}, bf16[256,2048]{1,0:T(8,128)(2,1)}, u32[]{:S(2)}) copy-start(bf16[256,2048]{1,0:T(8,128)(2,1)} %get-tuple-element.20) | copy-start | bytes 3145732
  191.0 6.0 %copy-start.12 = (bf16[256,2048]{1,0:T(8,128)(2,1)S(1)}, bf16[256,2048]{1,0:T(8,128)(2,1)}, u32[]{:S(2)}) copy-start(bf16[256,2048]{1,0:T(8,128)(2,1)} %get-tuple-element.22) | copy-start | bytes 3145732
  193.0 9.2 %collective-permute-start.26 = (bf16[336,512]{1,0:T(8,128)(2,1)S(1)}, bf16[336,512]{1,0:T(8,128)(2,1)S(1)}, u32[]{:S(2)}, u32[]{:S(2)}) collective-permute-start(bf16[336,512]{1,0:T(8,128)(2,1)S(1)} %get-tuple-element.36), channel_id=1, source_target_pairs={{0,24},{2,26},{4,28},{6,30},{8,0},{10,2},{12,4},{14,6},{16,8},{18,... | collective-permute-start | bytes 1032200 | tf_op jit(solution)/shard_map/ppermute | solution.py:362
  193.1 25.0 %collective-permute-start.25 = (bf16[336,512]{1,0:T(8,128)(2,1)S(1)}, bf16[336,512]{1,0:T(8,128)(2,1)S(1)}, u32[]{:S(2)}, u32[]{:S(2)}) collective-permute-start(bf16[336,512]{1,0:T(8,128)(2,1)S(1)} %get-tuple-element.37), channel_id=1, source_target_pairs={{0,16},{2,18},{4,20},{6,22},{8,24},{10,26},{12,28},{14,30},{16,0},... | collective-permute-start | bytes 1032200 | tf_op jit(solution)/shard_map/ppermute | solution.py:362
  195.7 29.7 %collective-permute-start.24 = (bf16[336,512]{1,0:T(8,128)(2,1)S(1)}, bf16[336,512]{1,0:T(8,128)(2,1)S(1)}, u32[]{:S(2)}, u32[]{:S(2)}) collective-permute-start(bf16[336,512]{1,0:T(8,128)(2,1)S(1)} %get-tuple-element.35), channel_id=1, source_target_pairs={{0,8},{2,10},{4,12},{6,14},{8,16},{10,18},{12,20},{14,22},{16,24},... | collective-permute-start | bytes 1032200 | tf_op jit(solution)/shard_map/ppermute | solution.py:362
  197.0 28.7 %copy-start.9 = (bf16[1,256,1024]{2,1,0:T(8,128)(2,1)}, bf16[1,256,1024]{2,1,0:T(8,128)(2,1)S(1)}, u32[]{:S(2)}) copy-start(bf16[1,256,1024]{2,1,0:T(8,128)(2,1)S(1)} %bitcast_dynamic-update-slice_fusion.1) | copy-start | bytes 1572868
  197.2 29.4 %copy-start.11 = (bf16[1,256,2048]{2,1,0:T(8,128)(2,1)}, bf16[1,256,2048]{2,1,0:T(8,128)(2,1)S(1)}, u32[]{:S(2)}) copy-start(bf16[1,256,2048]{2,1,0:T(8,128)(2,1)S(1)} %get-tuple-element.39) | copy-start | bytes 3145732
  197.2 29.4 %copy-start.13 = (bf16[1,256,2048]{2,1,0:T(8,128)(2,1)}, bf16[1,256,2048]{2,1,0:T(8,128)(2,1)S(1)}, u32[]{:S(2)}) copy-start(bf16[1,256,2048]{2,1,0:T(8,128)(2,1)S(1)} %get-tuple-element.38) | copy-start | bytes 3145732
  225.7 1.8 collective-permute-start.27
  226.6 1.5 copy-start.6
  227.6 0.9 copy-start.8

commit v3 on v2

--- a/solution.py
+++ b/solution.py
@@ -189,8 +189,8 @@
         + [jax.ShapeDtypeStruct((rows, width), BF16)] * n_arr,
         compiler_params=pltpu.CompilerParams(vmem_limit_bytes=40 * 1024 * 1024),
         cost_estimate=pl.CostEstimate(
-            flops=heads * 2 * span * lanes * HD * 2 * 2 * 6,
-            bytes_accessed=heads * 2 * span * lanes * 2,
+            flops=heads * 2 * span * lanes * HD // 16,
+            bytes_accessed=heads * span * lanes // 16,
             transcendentals=0,
         ),
         name="probs",
@@ -226,8 +226,8 @@
         + [jax.ShapeDtypeStruct((rows, width), BF16)] * n_arr,
         compiler_params=pltpu.CompilerParams(vmem_limit_bytes=40 * 1024 * 1024),
         cost_estimate=pl.CostEstimate(
-            flops=heads * 2 * span * lanes * HD * 2 * 4 * 4,
-            bytes_accessed=heads * 2 * span * lanes * 2,
+            flops=heads * 2 * span * lanes * HD // 16,
+            bytes_accessed=heads * span * lanes // 16,
             transcendentals=0,
         ),
         name="grads",
@@ -377,9 +377,11 @@
     out, dq, other, *dk_terms = run_grads(
         core_arg, e, inv, do_t, queries[0], q_other, keys, vals, chip_rows, half_kv
     )
+    dk_back = [shifted(dk_terms[n_back - d], -2 * d) for d in range(1, n_back + 1)]
+    dk_back, by_z = lax.optimization_barrier((dk_back, by_z))
     dk_total = dk_terms[n_back].astype(F32)
-    for d in range(1, n_back + 1):
-        dk_total = dk_total + shifted(dk_terms[n_back - d], -2 * d).astype(F32)
+    for term in dk_back:
+        dk_total = dk_total + term.astype(F32)
     dk_chip = dk_total.astype(BF16)
     d_keys = placed(core, rows_of(dk_chip, core, shard_rows), swapped(rows_of(dk_chip, 1 - core, shard_rows)), 1)
     other = swapped(other)

time: 232 us -> 226 us (0.974)
  waiting for transfers between devices: 100 us -> 93.4 us
    ppermute x8, waiting for transfers between devices: 50.1 us -> 43.3 us  [shifted(): lax.ppermute(x, 'ctx', [(i, i + by) for i in range(length) if 0 <= i + by...]
  transfers between devices with their start and end apart: 28 -> 28, of which waited for: 15 -> 15; matrix products, arithmetic and copies ran while one was open for 17% -> 18% of each run, Pallas kernels for 13% -> 14%
where the time goes in v3:
time: 226 us; the launch traced here: 223 us
  waiting for transfers between devices  93.4 us (41%)
  starting transfers between devices  53.5 us (24%)
  Pallas kernels  30.3 us (13%)
  matrix products  22.1 us (10%)
  local copies, waits for them, and re-layouts  15 us (7%)
  other arithmetic  7.04 us (3%)
    ppermute x8, waiting for transfers between devices, shifted(): lax.ppermute(x, 'ctx', [(i, i + by) for i in range(length) if 0 <= i + by...  43.3 us
    ppermute x3, waiting for transfers between devices, shards(): lax.ppermute(piece, 'ctx', [(i, (i + 4 * d) % n_ctx) for i in range(n_ctx)])  28.2 us
    ppermute x8, starting transfers between devices, shifted(): lax.ppermute(x, 'ctx', [(i, i + by) for i in range(length) if 0 <= i + by...  27.8 us
    dot_general x11, matrix products, dot(): return lax.dot_general(a, b, dims, preferred_element_type=F32)  22.1 us
    pallas_call x1, Pallas kernels, run_grads(): pl.pallas_call(functools.partial(grads_kernel, blk, n_arr - 1), grid_spec...  15.9 us
    pallas_call x1, Pallas kernels, run_probs(): pl.pallas_call(functools.partial(probs_kernel, blk, n_arr - 1), grid_spec...  14.4 us
    ppermute x8, starting transfers between devices, swapped(): lax.ppermute(x, 'ctx', [(i, i ^ 1) for i in range(lax.axis_size('ctx'))])  13.2 us
    ppermute x6, waiting for transfers between devices, moved(): return lax.ppermute(x, ('ctx', 'fsdp'), pairs)  12.1 us
  transfers between devices with their start and end apart: 28, of which 15 were waited for; matrix products, arithmetic and copies ran while one was open for 18% of the time, Pallas kernels for 14%

profile of v3, /device:TPU:9, one launch (start us, length us, event | category | flops | bytes accessed | tf_op | source)
XLA Modules:
  0.0 222.6 jit_solution(4602561469583814439)
XLA Ops:
  1.4 1.1 dynamic-slice_bitcast_fusion.7
  3.4 1.3 dynamic-slice_bitcast_fusion.1
  4.6 1.1 pad_maximum_fusion.1
  5.9 3.1 %collective-permute-start.2 = (bf16[528,512]{1,0:T(8,128)(2,1)S(1)}, bf16[528,512]{1,0:T(8,128)(2,1)S(1)}, u32[]{:S(2)}, u32[]{:S(2)}) collective-permute-start(bf16[528,512]{1,0:T(8,128)(2,1)S(1)} %pad_maximum_fusion.3.refs_2_), channel_id=1, source_target_pairs={{0,4},{2,6},{4,8},{6,10},{8,12},{10,14},{12,16},{14,18},{16,20},{1... | collective-permute-start | bytes 1622024 | tf_op jit(solution)/shard_map/ppermute | solution.py:239
  9.0 3.2 %collective-permute-start.1 = (bf16[528,512]{1,0:T(8,128)(2,1)S(1)}, bf16[528,512]{1,0:T(8,128)(2,1)}, u32[]{:S(2)}, u32[]{:S(2)}) collective-permute-start(bf16[528,512]{1,0:T(8,128)(2,1)S(1)} %pad_maximum_fusion.3.refs_2_), channel_id=1, source_target_pairs={{0,8},{2,10},{4,12},{6,14},{8,16},{10,18},{12,20},{14,22},{16,24},... | collective-permute-start | bytes 1622024 | tf_op jit(solution)/shard_map/ppermute | solution.py:239
  12.2 2.5 %dynamic-slice_bitcast_fusion = bf16[256,2688]{1,0:T(8,128)(2,1)} fusion(bf16[1,256,5376]{2,1,0:T(8,128)(2,1)} %param.6, s32[]{:T(128)S(6)} %select_n.145), kind=kLoop, calls=%fused_computation.15 | loop fusion | bytes 2752516 | tf_op jit(solution)/shard_map/dynamic_slice | solution.py:262
  14.8 1.2 collective-permute-start.4
  16.0 4.6 %copy.12 = bf16[1,256,5376]{1,2,0:T(8,128)(2,1)} copy(bf16[1,256,5376]{2,1,0:T(8,128)(2,1)} %param.6) | data formatting | bytes 5505024 | tf_op args[0]
  20.6 1.4 collective-permute-done.2.refs_1_
  22.1 2.0 collective-permute-done.1.refs_0_
  25.5 1.2 copy-done.1
  26.7 14.4 %probs.1 = (bf16[4,2,1280,512]{3,2,1,0:T(8,128)(2,1)}, f32[4,2,1,512]{3,2,1,0:T(1,128)S(1)}, bf16[4,2,128,512]{3,2,1,0:T(8,128)(2,1)S(1)}, bf16[512,512]{1,0:T(8...) custom-call(s32[1]{0:T(128)} %bitcast.core_ref, s32[1,512]{1,0:T(1,128)S(1)} %add_maximum_fusion.low_ref, ...), custom_call_target="tpu_custom_call" | custom-call | flops 41943040 | bytes 163840 | tf_op jit(solution)/shard_map/probs/pallas_call | solution.py:157
  41.1 1.9 collective-permute-start.13
  43.1 10.1 %collective-permute-start.12 = (bf16[512,512]{1,0:T(8,128)(2,1)}, bf16[512,512]{1,0:T(8,128)(2,1)}, u32[]{:S(2)}, u32[]{:S(2)}) collective-permute-start(bf16[512,512]{1,0:T(8,128)(2,1)} %get-tuple-element.29), channel_id=1, source_target_pairs={{4,0},{6,2},{8,4},{10,6},{12,8},{14,10},{16,12},{18,14},{20,16},{2... | collective-permute-start | bytes 1572872 | tf_op jit(solution)/shard_map/ppermute | solution.py:239
  53.2 1.6 constant_dynamic-slice_fusion.11
  54.8 2.7 %collective-permute-start.16 = (bf16[1344,256]{1,0:T(8,128)(2,1)}, bf16[1344,256]{1,0:T(8,128)(2,1)}, u32[]{:S(2)}, u32[]{:S(2)}) collective-permute-start(bf16[1344,256]{1,0:T(8,128)(2,1)} %bitcast.20), channel_id=1, source_target_pairs={{0,5},{1,4},{2,7},{3,6},{4,1},{5,0},{6,3},{7,2},{8,13},{9,12},{10,... | collective-permute-start | bytes 2064392 | tf_op jit(solution)/shard_map/ppermute | solution.py:258
  57.5 4.7 %fusion.4 = f32[256,1024]{1,0:T(8,128)S(1)} fusion(bf16[2688,1024]{1,0:T(8,128)(2,1)} %param.9, bf16[1,256,5376]{2,1,0:T(8,128)(2,1)} %param.6, s32[]{:T(128)S(6)} %select_n.143), kind=kOutput, calls=%fused_computation.13 | convolution fusion | flops 1409286144 | bytes 7929860 | tf_op jit(solution)/shard_map/dot_general | solution.py:28
  62.7 18.2 %collective-permute-done.12 = bf16[512,512]{1,0:T(8,128)(2,1)} collective-permute-done((bf16[512,512]{1,0:T(8,128)(2,1)}, bf16[512,512]{1,0:T(8,128)(2,1)}, u32[]{:S(2)}, u32[]{:S(2)}) %collective-permute-start.12) | collective-permute-done | bytes 524320 | tf_op jit(solution)/shard_map/ppermute | solution.py:239
  80.9 1.4 add_convert_fusion.1
  82.3 1.3 collective-permute-start.18
  83.6 4.6 %convolution_convert_fusion.1 = bf16[256,1024]{1,0:T(8,128)(2,1)S(1)} fusion(bf16[256,2688]{1,0:T(8,128)(2,1)} %collective-permute-done.4, bf16[2688,1024]{1,0:T(8,128)(2,1)} %param.9), kind=kOutput, calls=%fused_computation.17 | convolution fusion | flops 1409548288 | bytes 7405568 | tf_op jit(solution)/shard_map/dot_general | solution.py:28
  88.5 8.7 %collective-permute-done.15 = bf16[1344,256]{1,0:T(8,128)(2,1)} collective-permute-done((bf16[1344,256]{1,0:T(8,128)(2,1)}, bf16[1344,256]{1,0:T(8,128)(2,1)}, u32[]{:S(2)}, u32[]{:S(2)}) %collective-permute-start.15) | collective-permute-done | bytes 688160 | tf_op jit(solution)/shard_map/ppermute | solution.py:258
  97.2 2.1 pad_maximum_fusion
  99.4 2.9 %collective-permute-start.17 = (bf16[1344,1024]{1,0:T(8,128)(2,1)S(1)}, bf16[1344,1024]{1,0:T(8,128)(2,1)S(1)}, u32[]{:S(2)}, u32[]{:S(2)}) collective-permute-start(bf16[1344,1024]{1,0:T(8,128)(2,1)S(1)} %pad_maximum_fusion), channel_id=1, source_target_pairs={{0,2},{2,0},{4,6},{6,4},{8,10},{10,8},{12,14},{14,12},{16,18},{18,... | collective-permute-start | bytes 8257544 | tf_op jit(solution)/shard_map/ppermute | solution.py:243
  103.1 1.6 collective-permute-start.19
  104.7 3.4 %collective-permute-done.18 = bf16[512,512]{1,0:T(8,128)(2,1)S(1)} collective-permute-done((bf16[512,512]{1,0:T(8,128)(2,1)S(1)}, bf16[512,512]{1,0:T(8,128)(2,1)S(1)}, u32[]{:S(2)}, u32[]{:S(2)}) %collective-permute-start.18) | collective-permute-done | bytes 524320 | tf_op jit(solution)/shard_map/ppermute | solution.py:258
  108.2 3.3 %collective-permute-start.22 = (bf16[512,512]{1,0:T(8,128)(2,1)S(1)}, bf16[512,512]{1,0:T(8,128)(2,1)S(1)}, u32[]{:S(2)}, u32[]{:S(2)}) collective-permute-start(bf16[512,512]{1,0:T(8,128)(2,1)S(1)} %pad_maximum_fusion.6), channel_id=1, source_target_pairs={{0,2},{2,0},{4,6},{6,4},{8,10},{10,8},{12,14},{14,12},{16,18},{18,... | collective-permute-start | bytes 1572872 | tf_op jit(solution)/shard_map/ppermute | solution.py:243
  111.5 7.8 %collective-permute-done.5 = bf16[256,1024]{1,0:T(8,128)(2,1)S(1)} collective-permute-done((bf16[256,1024]{1,0:T(8,128)(2,1)S(1)}, bf16[256,1024]{1,0:T(8,128)(2,1)S(1)}, u32[]{:S(2)}, u32[]{:S(2)}) %collective-permute-start.5) | collective-permute-done | bytes 524320 | tf_op jit(solution)/shard_map/ppermute | solution.py:248
  119.5 3.3 %collective-permute-start.6 = (bf16[256,512]{1,0:T(8,128)(2,1)S(1)}, bf16[256,512]{1,0:T(8,128)(2,1)S(1)}, u32[]{:S(2)}, u32[]{:S(2)}) collective-permute-start(bf16[256,512]{1,0:T(8,128)(2,1)S(1)} %get-tuple-element.52), channel_id=1, source_target_pairs={{0,2},{2,0},{4,6},{6,4},{8,10},{10,8},{12,14},{14,12},{16,18},{18,... | collective-permute-start | bytes 786440 | tf_op jit(solution)/shard_map/ppermute | solution.py:243
  123.0 1.0 collective-permute-done.6
  124.0 3.5 %collective-permute-start.7 = (bf16[512,512]{1,0:T(8,128)(2,1)S(1)}, bf16[512,512]{1,0:T(8,128)(2,1)S(1)}, u32[]{:S(2)}, u32[]{:S(2)}) collective-permute-start(bf16[512,512]{1,0:T(8,128)(2,1)S(1)} %constant_dynamic-update-slice_fusion.2.refs_5_), channel_id=1, source_target_pairs={{0,8},{2,10},{4,12},{6,14},{8,16},{10,18},{12,20},{14,22},{16,24},... | collective-permute-start | bytes 1572872 | tf_op jit(solution)/shard_map/ppermute | solution.py:239
  127.6 2.1 collective-permute-start.8
  129.8 6.0 %convolution_convert_fusion = bf16[512,2688]{1,0:T(8,128)(2,1)S(1)} fusion(bf16[512,1024]{1,0:T(8,128)(2,1)S(1)} %constant_dynamic-update-slice_fusion.1, bf16[2688,1024]{1,0:T(8,128)(2,1)} %param.9), kind=kOutput, calls=%fused_computation | convolution fusion | flops 2819948544 | bytes 9306112 | tf_op jit(solution)/shard_map/dot_general | solution.py:28
  136.2 2.9 %collective-permute-done.7.refs_3_ = bf16[512,512]{1,0:T(8,128)(2,1)S(1)} collective-permute-done((bf16[512,512]{1,0:T(8,128)(2,1)S(1)}, bf16[512,512]{1,0:T(8,128)(2,1)S(1)}, u32[]{:S(2)}, u32[]{:S(2)}) %collective-permute-start.7) | collective-permute-done | bytes 524320 | tf_op jit(solution)/shard_map/ppermute | solution.py:239
  139.1 1.2 collective-permute-start.23
  140.3 2.9 %collective-permute-done.8.refs_4_ = bf16[512,512]{1,0:T(8,128)(2,1)S(1)} collective-permute-done((bf16[512,512]{1,0:T(8,128)(2,1)S(1)}, bf16[512,512]{1,0:T(8,128)(2,1)S(1)}, u32[]{:S(2)}, u32[]{:S(2)}) %collective-permute-start.8) | collective-permute-done | bytes 524320 | tf_op jit(solution)/shard_map/ppermute | solution.py:239
  143.2 15.9 %grads.1 = (bf16[256,2048]{1,0:T(8,128)(2,1)}, bf16[256,2048]{1,0:T(8,128)(2,1)}, bf16[2,256,1024]{2,1,0:T(8,128)(2,1)S(1)}, bf16[512,512]{1,0:T(8,128)(2,1)S(1)...) custom-call(s32[1]{0:T(128)} %bitcast.core_ref, bf16[4,2,1280,512]{3,2,1,0:T(8,128)(2,1)} %get-tuple-element.19.e_ref, ...), custom_call_target="tpu_custom_call" | custom-call | flops 41943040 | bytes 163840 | tf_op jit(solution)/shard_map/grads/pallas_call | solution.py:204
  159.1 1.6 collective-permute-start.9
  160.6 1.9 collective-permute-start.10
  163.6 1.9 collective-permute-start.11
  166.1 1.6 convolution_add_fusion
  169.4 1.9 fusion.3
  171.3 4.8 %collective-permute-done.10 = bf16[512,512]{1,0:T(8,128)(2,1)S(1)} collective-permute-done((bf16[512,512]{1,0:T(8,128)(2,1)S(1)}, bf16[512,512]{1,0:T(8,128)(2,1)S(1)}, u32[]{:S(2)}, u32[]{:S(2)}) %collective-permute-start.10) | collective-permute-done | bytes 524320 | tf_op jit(solution)/shard_map/ppermute | solution.py:239
  176.0 11.0 %collective-permute-done.11 = bf16[512,512]{1,0:T(8,128)(2,1)S(1)} collective-permute-done((bf16[512,512]{1,0:T(8,128)(2,1)S(1)}, bf16[512,512]{1,0:T(8,128)(2,1)S(1)}, u32[]{:S(2)}, u32[]{:S(2)}) %collective-permute-start.11) | collective-permute-done | bytes 524320 | tf_op jit(solution)/shard_map/ppermute | solution.py:239
  188.6 2.4 %collective-permute-start.25 = (bf16[336,512]{1,0:T(8,128)(2,1)S(1)}, bf16[336,512]{1,0:T(8,128)(2,1)S(1)}, u32[]{:S(2)}, u32[]{:S(2)}) collective-permute-start(bf16[336,512]{1,0:T(8,128)(2,1)S(1)} %get-tuple-element.41), channel_id=1, source_target_pairs={{0,16},{2,18},{4,20},{6,22},{8,24},{10,26},{12,28},{14,30},{16,0},... | collective-permute-start | bytes 1032200 | tf_op jit(solution)/shard_map/ppermute | solution.py:362
  191.5 6.6 %collective-permute-done.26 = bf16[336,512]{1,0:T(8,128)(2,1)S(1)} collective-permute-done((bf16[336,512]{1,0:T(8,128)(2,1)S(1)}, bf16[336,512]{1,0:T(8,128)(2,1)S(1)}, u32[]{:S(2)}, u32[]{:S(2)}) %collective-permute-start.26) | collective-permute-done | bytes 344096 | tf_op jit(solution)/shard_map/ppermute | solution.py:362
  198.0 14.3 %collective-permute-done.25 = bf16[336,512]{1,0:T(8,128)(2,1)S(1)} collective-permute-done((bf16[336,512]{1,0:T(8,128)(2,1)S(1)}, bf16[336,512]{1,0:T(8,128)(2,1)S(1)}, u32[]{:S(2)}, u32[]{:S(2)}) %collective-permute-start.25) | collective-permute-done | bytes 344096 | tf_op jit(solution)/shard_map/ppermute | solution.py:362
  212.3 7.4 %collective-permute-done.24 = bf16[336,512]{1,0:T(8,128)(2,1)S(1)} collective-permute-done((bf16[336,512]{1,0:T(8,128)(2,1)S(1)}, bf16[336,512]{1,0:T(8,128)(2,1)S(1)}, u32[]{:S(2)}, u32[]{:S(2)}) %collective-permute-start.24) | collective-permute-done | bytes 344096 | tf_op jit(solution)/shard_map/ppermute | solution.py:362
  (99 shorter events, 13.6 us)
Async XLA Ops:
  2.6 3.1 %collective-permute-start = (bf16[272,512]{1,0:T(8,128)(2,1)S(1)}, bf16[272,512]{1,0:T(8,128)(2,1)S(1)}, u32[]{:S(2)}, u32[]{:S(2)}) collective-permute-start(bf16[272,512]{1,0:T(8,128)(2,1)S(1)} %maximum_maximum_fusion.1), channel_id=1, source_target_pairs={{0,2},{2,0},{4,6},{6,4},{8,10},{10,8},{12,14},{14,12},{16,18},{18,... | collective-permute-start | bytes 835592 | tf_op jit(solution)/shard_map/ppermute | solution.py:243
  5.7 19.7 %collective-permute-start.3 = (bf16[256,2048]{1,0:T(8,128)(2,1)}, bf16[256,2048]{1,0:T(8,128)(2,1)S(1)}, u32[]{:S(2)}, u32[]{:S(2)}) collective-permute-start(bf16[256,2048]{1,0:T(8,128)(2,1)} %pad_maximum_fusion.1), channel_id=1, source_target_pairs={{0,2},{2,0},{4,6},{6,4},{8,10},{10,8},{12,14},{14,12},{16,18},{18,... | collective-permute-start | bytes 3145736 | tf_op jit(solution)/shard_map/ppermute | solution.py:243
  5.9 16.2 %collective-permute-start.2 = (bf16[528,512]{1,0:T(8,128)(2,1)S(1)}, bf16[528,512]{1,0:T(8,128)(2,1)S(1)}, u32[]{:S(2)}, u32[]{:S(2)}) collective-permute-start(bf16[528,512]{1,0:T(8,128)(2,1)S(1)} %pad_maximum_fusion.3.refs_2_), channel_id=1, source_target_pairs={{0,4},{2,6},{4,8},{6,10},{8,12},{10,14},{12,16},{14,18},{16,20},{1... | collective-permute-start | bytes 1622024 | tf_op jit(solution)/shard_map/ppermute | solution.py:239
  9.0 15.0 %collective-permute-start.1 = (bf16[528,512]{1,0:T(8,128)(2,1)S(1)}, bf16[528,512]{1,0:T(8,128)(2,1)}, u32[]{:S(2)}, u32[]{:S(2)}) collective-permute-start(bf16[528,512]{1,0:T(8,128)(2,1)S(1)} %pad_maximum_fusion.3.refs_2_), channel_id=1, source_target_pairs={{0,8},{2,10},{4,12},{6,14},{8,16},{10,18},{12,20},{14,22},{16,24},... | collective-permute-start | bytes 1622024 | tf_op jit(solution)/shard_map/ppermute | solution.py:239
  14.8 68.8 %collective-permute-start.4 = (bf16[256,2688]{1,0:T(8,128)(2,1)}, bf16[256,2688]{1,0:T(8,128)(2,1)}, u32[]{:S(2)}, u32[]{:S(2)}) collective-permute-start(bf16[256,2688]{1,0:T(8,128)(2,1)} %dynamic-slice_bitcast_fusion), channel_id=1, source_target_pairs={{0,1},{1,0},{2,3},{3,2},{4,5},{5,4},{6,7},{7,6},{8,9},{9,8},{10,11... | collective-permute-start | bytes 4128776 | tf_op jit(solution)/shard_map/ppermute | solution.py:248
  16.0 9.5 %copy-start = (bf16[1,256,2048]{2,1,0:T(8,128)(2,1)S(1)}, bf16[1,256,2048]{2,1,0:T(8,128)(2,1)}, u32[]{:S(2)}) copy-start(bf16[1,256,2048]{2,1,0:T(8,128)(2,1)} %param.7) | copy-start | bytes 3145732
  25.4 1.2 copy-start.1
  26.7 26.5 %copy-start.6 = (bf16[1,256,5376]{1,2,0:T(8,128)(2,1)S(1)}, bf16[1,256,5376]{1,2,0:T(8,128)(2,1)}, u32[]{:S(2)}) copy-start(bf16[1,256,5376]{1,2,0:T(8,128)(2,1)} %copy.12) | copy-start | bytes 8257540
  41.1 13.7 %copy-start.2 = (bf16[4,2,128,512]{3,2,1,0:T(8,128)(2,1)}, bf16[4,2,128,512]{3,2,1,0:T(8,128)(2,1)S(1)}, u32[]{:S(2)}) copy-start(bf16[4,2,128,512]{3,2,1,0:T(8,128)(2,1)S(1)} %get-tuple-element.21.dot_ref) | copy-start | bytes 3145732
  41.1 13.7 %copy-start.4 = (bf16[512,512]{1,0:T(8,128)(2,1)}, bf16[512,512]{1,0:T(8,128)(2,1)S(1)}, u32[]{:S(2)}) copy-start(bf16[512,512]{1,0:T(8,128)(2,1)S(1)} %get-tuple-element.28) | copy-start | bytes 1572868
  41.1 21.1 %collective-permute-start.13 = (bf16[512,512]{1,0:T(8,128)(2,1)}, bf16[512,512]{1,0:T(8,128)(2,1)}, u32[]{:S(2)}, u32[]{:S(2)}) collective-permute-start(bf16[512,512]{1,0:T(8,128)(2,1)} %get-tuple-element.30), channel_id=1, source_target_pairs={{8,0},{10,2},{12,4},{14,6},{16,8},{18,10},{20,12},{22,14},{24,16},... | collective-permute-start | bytes 1572872 | tf_op jit(solution)/shard_map/ppermute | solution.py:239
  43.1 37.8 %collective-permute-start.12 = (bf16[512,512]{1,0:T(8,128)(2,1)}, bf16[512,512]{1,0:T(8,128)(2,1)}, u32[]{:S(2)}, u32[]{:S(2)}) collective-permute-start(bf16[512,512]{1,0:T(8,128)(2,1)} %get-tuple-element.29), channel_id=1, source_target_pairs={{4,0},{6,2},{8,4},{10,6},{12,8},{14,10},{16,12},{18,14},{20,16},{2... | collective-permute-start | bytes 1572872 | tf_op jit(solution)/shard_map/ppermute | solution.py:239
  54.8 33.8 %collective-permute-start.16 = (bf16[1344,256]{1,0:T(8,128)(2,1)}, bf16[1344,256]{1,0:T(8,128)(2,1)}, u32[]{:S(2)}, u32[]{:S(2)}) collective-permute-start(bf16[1344,256]{1,0:T(8,128)(2,1)} %bitcast.20), channel_id=1, source_target_pairs={{0,5},{1,4},{2,7},{3,6},{4,1},{5,0},{6,3},{7,2},{8,13},{9,12},{10,... | collective-permute-start | bytes 2064392 | tf_op jit(solution)/shard_map/ppermute | solution.py:258
  57.5 39.8 %collective-permute-start.15 = (bf16[1344,256]{1,0:T(8,128)(2,1)}, bf16[1344,256]{1,0:T(8,128)(2,1)}, u32[]{:S(2)}, u32[]{:S(2)}) collective-permute-start(bf16[1344,256]{1,0:T(8,128)(2,1)} %bitcast.19), channel_id=1, source_target_pairs={{0,4},{1,5},{2,6},{3,7},{4,0},{5,1},{6,2},{7,3},{8,12},{9,13},{10,... | collective-permute-start | bytes 2064392 | tf_op jit(solution)/shard_map/ppermute | solution.py:258
  57.5 4.7 %copy-start.9 = (bf16[4,1,2,1,168,256]{5,4,3,2,1,0:T(8,128)(2,1)S(1)}, bf16[4,1,2,1,168,256]{5,4,3,2,1,0:T(8,128)(2,1)}, u32[]{:S(2)}) copy-start(bf16[4,1,2,1,168,256]{5,4,3,2,1,0:T(8,128)(2,1)} %get-tuple-element.38) | copy-start | bytes 2064388
  57.5 23.4 %copy-start.5 = (bf16[512,512]{1,0:T(8,128)(2,1)S(1)}, bf16[512,512]{1,0:T(8,128)(2,1)}, u32[]{:S(2)}) copy-start(bf16[512,512]{1,0:T(8,128)(2,1)} %copy-done.4) | copy-start | bytes 1572868
  62.2 35.0 %collective-permute-start.14 = (bf16[1344,256]{1,0:T(8,128)(2,1)S(1)}, bf16[1344,256]{1,0:T(8,128)(2,1)S(1)}, u32[]{:S(2)}, u32[]{:S(2)}) collective-permute-start(bf16[1344,256]{1,0:T(8,128)(2,1)S(1)} %bitcast.67), channel_id=1, source_target_pairs={{0,1},{1,0},{2,3},{3,2},{4,5},{5,4},{6,7},{7,6},{8,9},{9,8},{10,11... | collective-permute-start | bytes 2064392 | tf_op jit(solution)/shard_map/ppermute | solution.py:258
  82.3 15.0 %copy-start.7 = (bf16[4,1,2,1,168,256]{5,4,3,2,1,0:T(8,128)(2,1)S(1)}, bf16[4,1,2,1,168,256]{5,4,3,2,1,0:T(8,128)(2,1)}, u32[]{:S(2)}) copy-start(bf16[4,1,2,1,168,256]{5,4,3,2,1,0:T(8,128)(2,1)} %get-tuple-element.35) | copy-start | bytes 2064388
  82.3 25.8 %collective-permute-start.18 = (bf16[512,512]{1,0:T(8,128)(2,1)S(1)}, bf16[512,512]{1,0:T(8,128)(2,1)S(1)}, u32[]{:S(2)}, u32[]{:S(2)}) collective-permute-start(bf16[512,512]{1,0:T(8,128)(2,1)S(1)} %add_convert_fusion.1), channel_id=1, source_target_pairs={{0,1},{1,0},{2,3},{3,2},{4,5},{5,4},{6,7},{7,6},{8,9},{9,8},{10,11... | collective-permute-start | bytes 1572872 | tf_op jit(solution)/shard_map/ppermute | solution.py:258
  88.2 31.1 %collective-permute-start.5 = (bf16[256,1024]{1,0:T(8,128)(2,1)S(1)}, bf16[256,1024]{1,0:T(8,128)(2,1)S(1)}, u32[]{:S(2)}, u32[]{:S(2)}) collective-permute-start(bf16[256,1024]{1,0:T(8,128)(2,1)S(1)} %convolution_convert_fusion.1), channel_id=1, source_target_pairs={{0,1},{1,0},{2,3},{3,2},{4,5},{5,4},{6,7},{7,6},{8,9},{9,8},{10,11... | collective-permute-start | bytes 1572872 | tf_op jit(solution)/shard_map/ppermute | solution.py:248
  99.4 61.3 %collective-permute-start.17 = (bf16[1344,1024]{1,0:T(8,128)(2,1)S(1)}, bf16[1344,1024]{1,0:T(8,128)(2,1)S(1)}, u32[]{:S(2)}, u32[]{:S(2)}) collective-permute-start(bf16[1344,1024]{1,0:T(8,128)(2,1)S(1)} %pad_maximum_fusion), channel_id=1, source_target_pairs={{0,2},{2,0},{4,6},{6,4},{8,10},{10,8},{12,14},{14,12},{16,18},{18,... | collective-permute-start | bytes 8257544 | tf_op jit(solution)/shard_map/ppermute | solution.py:243
  102.3 61.3 %collective-permute-start.20 = (bf16[512,512]{1,0:T(8,128)(2,1)S(1)}, bf16[512,512]{1,0:T(8,128)(2,1)S(1)}, u32[]{:S(2)}, u32[]{:S(2)}) collective-permute-start(bf16[512,512]{1,0:T(8,128)(2,1)S(1)} %add_convert_fusion.1), channel_id=1, source_target_pairs={{0,5},{1,4},{2,7},{3,6},{4,1},{5,0},{6,3},{7,2},{8,13},{9,12},{10,... | collective-permute-start | bytes 1572872 | tf_op jit(solution)/shard_map/ppermute | solution.py:258
  103.1 65.8 %collective-permute-start.19 = (bf16[512,512]{1,0:T(8,128)(2,1)S(1)}, bf16[512,512]{1,0:T(8,128)(2,1)S(1)}, u32[]{:S(2)}, u32[]{:S(2)}) collective-permute-start(bf16[512,512]{1,0:T(8,128)(2,1)S(1)} %add_convert_fusion.1), channel_id=1, source_target_pairs={{0,4},{1,5},{2,6},{3,7},{4,0},{5,1},{6,2},{7,3},{8,12},{9,13},{10,... | collective-permute-start | bytes 1572872 | tf_op jit(solution)/shard_map/ppermute | solution.py:258
  108.2 19.4 %collective-permute-start.22 = (bf16[512,512]{1,0:T(8,128)(2,1)S(1)}, bf16[512,512]{1,0:T(8,128)(2,1)S(1)}, u32[]{:S(2)}, u32[]{:S(2)}) collective-permute-start(bf16[512,512]{1,0:T(8,128)(2,1)S(1)} %pad_maximum_fusion.6), channel_id=1, source_target_pairs={{0,2},{2,0},{4,6},{6,4},{8,10},{10,8},{12,14},{14,12},{16,18},{18,... | collective-permute-start | bytes 1572872 | tf_op jit(solution)/shard_map/ppermute | solution.py:243
  119.5 4.5 %collective-permute-start.6 = (bf16[256,512]{1,0:T(8,128)(2,1)S(1)}, bf16[256,512]{1,0:T(8,128)(2,1)S(1)}, u32[]{:S(2)}, u32[]{:S(2)}) collective-permute-start(bf16[256,512]{1,0:T(8,128)(2,1)S(1)} %get-tuple-element.52), channel_id=1, source_target_pairs={{0,2},{2,0},{4,6},{6,4},{8,10},{10,8},{12,14},{14,12},{16,18},{18,... | collective-permute-start | bytes 786440 | tf_op jit(solution)/shard_map/ppermute | solution.py:243
  124.0 15.0 %collective-permute-start.7 = (bf16[512,512]{1,0:T(8,128)(2,1)S(1)}, bf16[512,512]{1,0:T(8,128)(2,1)S(1)}, u32[]{:S(2)}, u32[]{:S(2)}) collective-permute-start(bf16[512,512]{1,0:T(8,128)(2,1)S(1)} %constant_dynamic-update-slice_fusion.2.refs_5_), channel_id=1, source_target_pairs={{0,8},{2,10},{4,12},{6,14},{8,16},{10,18},{12,20},{14,22},{16,24},... | collective-permute-start | bytes 1572872 | tf_op jit(solution)/shard_map/ppermute | solution.py:239
  127.6 15.6 %collective-permute-start.8 = (bf16[512,512]{1,0:T(8,128)(2,1)S(1)}, bf16[512,512]{1,0:T(8,128)(2,1)S(1)}, u32[]{:S(2)}, u32[]{:S(2)}) collective-permute-start(bf16[512,512]{1,0:T(8,128)(2,1)S(1)} %constant_dynamic-update-slice_fusion.2.refs_5_), channel_id=1, source_target_pairs={{0,4},{2,6},{4,8},{6,10},{8,12},{10,14},{12,16},{14,18},{16,20},{1... | collective-permute-start | bytes 1572872 | tf_op jit(solution)/shard_map/ppermute | solution.py:239
  136.0 7.2 %copy-start.3 = (bf16[4,2,128,512]{3,2,1,0:T(8,128)(2,1)S(1)}, bf16[4,2,128,512]{3,2,1,0:T(8,128)(2,1)}, u32[]{:S(2)}) copy-start(bf16[4,2,128,512]{3,2,1,0:T(8,128)(2,1)} %copy-done.2) | copy-start | bytes 3145732
  139.1 81.4 %collective-permute-start.23 = (bf16[256,2688]{1,0:T(8,128)(2,1)S(1)}, bf16[256,2688]{1,0:T(8,128)(2,1)S(1)}, u32[]{:S(2)}, u32[]{:S(2)}) collective-permute-start(bf16[256,2688]{1,0:T(8,128)(2,1)S(1)} %get-tuple-element.33), channel_id=1, source_target_pairs={{0,1},{1,0},{2,3},{3,2},{4,5},{5,4},{6,7},{7,6},{8,9},{9,8},{10,11... | collective-permute-start | bytes 4128776 | tf_op jit(solution)/shard_map/ppermute | solution.py:248
  159.1 32.2 %collective-permute-start.9 = (bf16[2,256,1024]{2,1,0:T(8,128)(2,1)S(1)}, bf16[2,256,1024]{2,1,0:T(8,128)(2,1)S(1)}, u32[]{:S(2)}, u32[]{:S(2)}) collective-permute-start(bf16[2,256,1024]{2,1,0:T(8,128)(2,1)S(1)} %get-tuple-element.23), channel_id=1, source_target_pairs={{0,2},{2,0},{4,6},{6,4},{8,10},{10,8},{12,14},{14,12},{16,18},{18,... | collective-permute-start | bytes 3145736 | tf_op jit(solution)/shard_map/ppermute | solution.py:243
  160.6 15.4 %collective-permute-start.10 = (bf16[512,512]{1,0:T(8,128)(2,1)S(1)}, bf16[512,512]{1,0:T(8,128)(2,1)S(1)}, u32[]{:S(2)}, u32[]{:S(2)}) collective-permute-start(bf16[512,512]{1,0:T(8,128)(2,1)S(1)} %get-tuple-element.26), channel_id=1, source_target_pairs={{4,0},{6,2},{8,4},{10,6},{12,8},{14,10},{16,12},{18,14},{20,16},{2... | collective-permute-start | bytes 1572872 | tf_op jit(solution)/shard_map/ppermute | solution.py:239
  163.6 23.5 %collective-permute-start.11 = (bf16[512,512]{1,0:T(8,128)(2,1)S(1)}, bf16[512,512]{1,0:T(8,128)(2,1)S(1)}, u32[]{:S(2)}, u32[]{:S(2)}) collective-permute-start(bf16[512,512]{1,0:T(8,128)(2,1)S(1)} %get-tuple-element.27), channel_id=1, source_target_pairs={{8,0},{10,2},{12,4},{14,6},{16,8},{18,10},{20,12},{22,14},{24,16},... | collective-permute-start | bytes 1572872 | tf_op jit(solution)/shard_map/ppermute | solution.py:239
  187.1 4.2 %copy-start.12 = (bf16[256,2048]{1,0:T(8,128)(2,1)S(1)}, bf16[256,2048]{1,0:T(8,128)(2,1)}, u32[]{:S(2)}) copy-start(bf16[256,2048]{1,0:T(8,128)(2,1)} %get-tuple-element.22) | copy-start | bytes 3145732
  187.1 4.2 %copy-start.14 = (bf16[256,2048]{1,0:T(8,128)(2,1)S(1)}, bf16[256,2048]{1,0:T(8,128)(2,1)}, u32[]{:S(2)}) copy-start(bf16[256,2048]{1,0:T(8,128)(2,1)} %get-tuple-element.24) | copy-start | bytes 3145732
  187.3 3.7 %collective-permute-start.21 = (bf16[256,512]{1,0:T(8,128)(2,1)S(1)}, bf16[256,512]{1,0:T(8,128)(2,1)S(1)}, u32[]{:S(2)}, u32[]{:S(2)}) collective-permute-start(bf16[256,512]{1,0:T(8,128)(2,1)S(1)} %get-tuple-element.46), channel_id=1, source_target_pairs={{0,2},{2,0},{4,6},{6,4},{8,10},{10,8},{12,14},{14,12},{16,18},{18,... | collective-permute-start | bytes 786440 | tf_op jit(solution)/shard_map/ppermute | solution.py:243
  188.3 9.7 %collective-permute-start.26 = (bf16[336,512]{1,0:T(8,128)(2,1)S(1)}, bf16[336,512]{1,0:T(8,128)(2,1)S(1)}, u32[]{:S(2)}, u32[]{:S(2)}) collective-permute-start(bf16[336,512]{1,0:T(8,128)(2,1)S(1)} %get-tuple-element.40), channel_id=1, source_target_pairs={{0,24},{2,26},{4,28},{6,30},{8,0},{10,2},{12,4},{14,6},{16,8},{18,... | collective-permute-start | bytes 1032200 | tf_op jit(solution)/shard_map/ppermute | solution.py:362
  188.6 23.7 %collective-permute-start.25 = (bf16[336,512]{1,0:T(8,128)(2,1)S(1)}, bf16[336,512]{1,0:T(8,128)(2,1)S(1)}, u32[]{:S(2)}, u32[]{:S(2)}) collective-permute-start(bf16[336,512]{1,0:T(8,128)(2,1)S(1)} %get-tuple-element.41), channel_id=1, source_target_pairs={{0,16},{2,18},{4,20},{6,22},{8,24},{10,26},{12,28},{14,30},{16,0},... | collective-permute-start | bytes 1032200 | tf_op jit(solution)/shard_map/ppermute | solution.py:362
  191.0 28.6 %collective-permute-start.24 = (bf16[336,512]{1,0:T(8,128)(2,1)S(1)}, bf16[336,512]{1,0:T(8,128)(2,1)S(1)}, u32[]{:S(2)}, u32[]{:S(2)}) collective-permute-start(bf16[336,512]{1,0:T(8,128)(2,1)S(1)} %get-tuple-element.39), channel_id=1, source_target_pairs={{0,8},{2,10},{4,12},{6,14},{8,16},{10,18},{12,20},{14,22},{16,24},... | collective-permute-start | bytes 1032200 | tf_op jit(solution)/shard_map/ppermute | solution.py:362
  191.3 28.6 %copy-start.11 = (bf16[1,256,1024]{2,1,0:T(8,128)(2,1)}, bf16[1,256,1024]{2,1,0:T(8,128)(2,1)S(1)}, u32[]{:S(2)}) copy-start(bf16[1,256,1024]{2,1,0:T(8,128)(2,1)S(1)} %bitcast_dynamic-update-slice_fusion.1) | copy-start | bytes 1572868
  191.4 29.3 %copy-start.13 = (bf16[1,256,2048]{2,1,0:T(8,128)(2,1)}, bf16[1,256,2048]{2,1,0:T(8,128)(2,1)S(1)}, u32[]{:S(2)}) copy-start(bf16[1,256,2048]{2,1,0:T(8,128)(2,1)S(1)} %get-tuple-element.43) | copy-start | bytes 3145732
  191.4 29.3 %copy-start.15 = (bf16[1,256,2048]{2,1,0:T(8,128)(2,1)}, bf16[1,256,2048]{2,1,0:T(8,128)(2,1)S(1)}, u32[]{:S(2)}) copy-start(bf16[1,256,2048]{2,1,0:T(8,128)(2,1)S(1)} %get-tuple-element.42) | copy-start | bytes 3145732
  219.9 1.8 collective-permute-start.27
  220.7 1.5 copy-start.8
  221.7 0.9 copy-start.10
